TPU v7x, 1024 devices: a whole 8x8x8 slice. The times are simulated.
1024 devices in a mesh: shard: 64 (over z, x), rep: 16 (over y, core).
Axes of the slice: x: 8, y: 8, z: 8, core: 2. Of those that a mesh axis runs over, the one named last changes fastest.
Arguments:
- emb_table: float32 [128, 2048, 256], P('shard'), may hold values from -0.4 to 0.4
- accumulated: float32 [128, 2048], P('shard'), may hold values from 500 to 20000
- touched: int32 [128, 512], P('shard'), may hold values from 0 to 2047, as said below
- bag_slots: int32 [128, 16, 2048, 16], P('shard', 'rep'), may hold values from 0 to 511
- lengths: int32 [128, 16, 2048], P('shard', 'rep'), may hold values from 1 to 16
- cotangent: bfloat16 [16, 2048, 128, 128], P('rep', 'shard'), may hold values from -6 to 6
Outputs:
- interaction: bfloat16 [16, 2048, 128, 128], P('rep', 'shard')
- new_rows: float32 [128, 512, 256], P('shard')
Inputs may be any that keep to these rules, and one draw needn't show every extreme that they name: `touched`: the 512 row ids of one table are distinct.
All inputs are finite; a program needn't handle non-finite values.
Results may differ from a plain program's by a relative error of at most 0.022.
Values may be sent and summed in bfloat16 or wider, within the bound.
A program may use at most 64 MiB of HBM per device.

v0:
```python
import jax
import jax.numpy as jnp
from jax import lax
from jax.sharding import PartitionSpec as P

learn_rate = 0.5
epsilon = 1e-08


def counts_block(slot_rows, length_rows, width):
    valid = jnp.arange(slot_rows.shape[-1], dtype=jnp.int32) < length_rows[..., None]
    hits = (slot_rows[..., None] == jnp.arange(width, dtype=jnp.int32)) & valid[..., None]
    return jnp.sum(hits.astype(jnp.int32), axis=-2).astype(jnp.bfloat16)


def adagrad_step(row_values, acc_values, gradient):
    acc_new = acc_values + jnp.mean(gradient * gradient, axis=-1)
    return row_values - learn_rate * gradient / (jnp.sqrt(acc_new)[..., None] + epsilon)


def local(emb_table, accumulated, touched, bag_slots, lengths, cotangent):
    tab_count, width = touched.shape
    table_rows = jnp.take_along_axis(emb_table, touched[:, :, None], axis=1)
    rows_low = table_rows.astype(jnp.bfloat16)
    slot_here = bag_slots[:, 0]
    len_here = lengths[:, 0]
    group_size = slot_here.shape[1]
    block_rows = 128
    block_count = group_size // block_rows

    def block_counts(pair):
        return counts_block(pair[0], pair[1], width)

    counts = lax.map(
        block_counts,
        (
            slot_here.reshape(tab_count * block_count, block_rows, slot_here.shape[2]),
            len_here.reshape(tab_count * block_count, block_rows),
        ),
    )
    counts = counts.reshape(tab_count, group_size, width)
    pooled = jnp.einsum(
        "tbk,tkd->tbd", counts, rows_low, preferred_element_type=jnp.float32
    ).astype(jnp.bfloat16)
    own_pooled = lax.all_to_all(pooled, "shard", split_axis=1, concat_axis=0, tiled=True)
    products = jnp.einsum(
        "tbd,sbd->bts", own_pooled, own_pooled, preferred_element_type=jnp.float32
    ).astype(jnp.bfloat16)
    cot_here = cotangent[0]
    dpool = (
        jnp.einsum("bts,sbd->tbd", cot_here, own_pooled, preferred_element_type=jnp.float32)
        + jnp.einsum("bst,sbd->tbd", cot_here, own_pooled, preferred_element_type=jnp.float32)
    ).astype(jnp.bfloat16)
    returned = lax.all_to_all(dpool, "shard", split_axis=0, concat_axis=1, tiled=True)
    gradient = jnp.einsum("tbk,tbd->tkd", counts, returned, preferred_element_type=jnp.float32)
    acc_rows = jnp.take_along_axis(accumulated, touched, axis=1)
    summed = lax.psum(gradient.astype(jnp.bfloat16), "rep").astype(jnp.float32)
    new_rows = adagrad_step(table_rows, acc_rows, summed)
    return (products[None], new_rows)


def solution(mesh):
    return jax.shard_map(
        local,
        mesh=mesh,
        in_specs=(
            P("shard", None, None),
            P("shard", None),
            P("shard", None),
            P("shard", "rep", None, None),
            P("shard", "rep", None),
            P("rep", "shard", None, None),
        ),
        out_specs=(P("rep", "shard", None, None), P("shard", None, None)),
        check_vma=False,
    )
```

profile of v0, /device:TPU:1, one launch (start us, length us, event | category | flops | bytes accessed | tf_op | source)
XLA Modules:
  0.0 464.5 jit_solution(7979463669074068069)
XLA Ops:
  10.0 142.2 %while.10 = (s32[]{:T(128)}, bf16[32,128,512]{2,1,0:T(8,128)(2,1)}, s32[32,128,16]{1,0,2:T(8,128)S(1)}, s32[32,128]{1,0:T(8,128)}, s32[]{:T(128)}) while((s32[]{:T(128)}, bf16[32,128,512]{2,1,0:T(8,128)(2,1)}, s32[32,128,16]{1,0,2:T(8,128)S(1)}, s32[32,128]{1,0:T(8,128)}, s32[]{:T(128)}) %tuple.30), condition=%wide.region_2.3_spmd, body=%wide.region_0.2_spmd.sunk | while | flops 4196354 | bytes 702533 | solution.py:34
  11.0 2.9 convert_reduce_fusion.2
  15.4 2.9 convert_reduce_fusion.2
  24.3 2.9 convert_reduce_fusion.2
  28.8 2.9 convert_reduce_fusion.2
  33.2 2.9 convert_reduce_fusion.2
  37.6 2.9 convert_reduce_fusion.2
  42.1 2.9 convert_reduce_fusion.2
  46.5 2.9 convert_reduce_fusion.2
  51.0 2.9 convert_reduce_fusion.2
  55.4 2.9 convert_reduce_fusion.2
  59.9 2.9 convert_reduce_fusion.2
  68.7 2.9 convert_reduce_fusion.2
  73.2 2.9 convert_reduce_fusion.2
  77.6 2.9 convert_reduce_fusion.2
  82.1 2.9 convert_reduce_fusion.2
  86.5 2.9 convert_reduce_fusion.2
  91.0 2.9 convert_reduce_fusion.2
  95.4 2.9 convert_reduce_fusion.2
  99.8 2.9 convert_reduce_fusion.2
  104.3 2.9 convert_reduce_fusion.2
  108.7 2.9 convert_reduce_fusion.2
  152.3 12.6 %gather_fusion = f32[1024,256]{1,0:T(8,128)S(1)} fusion(f32[2,2048,256]{2,1,0:T(8,128)} %param.8, s32[1024]{0:T(1024)S(1)} %bitcast.52), kind=kCustom, calls=%fused_computation | custom fusion | bytes 2105344 | tf_op jit(solution)/shard_map/jit(take_along_axis)/gather | solution.py:23
  165.0 3.9 convolution_convert_fusion
  168.9 12.8 %copy.35 = bf16[2,2048,256]{2,0,1:T(2,128)(2,1)S(1)} copy(bf16[2,2048,256]{2,1,0:T(8,128)(2,1)S(1)} %convolution_convert_fusion) | data formatting | bytes 4194304 | tf_op jit(solution)/shard_map/convert_element_type | solution.py:44
  181.7 72.2 %all_to_all.36 = bf16[2,2048,256]{2,0,1:T(2,128)(2,1)S(1)} all-to-all(bf16[2,2048,256]{2,0,1:T(2,128)(2,1)S(1)} %copy.35), channel_id=1, replica_groups=mesh['shard'=64,'rep'=16] {'shard'}, dimensions={1} | all-to-all | bytes 4194304 | tf_op jit(solution)/shard_map/all_to_all | solution.py:45
  253.9 3.5 copy.48
  263.2 4.6 copy.39
  267.8 11.3 %all-to-all-start.1 = ((bf16[128,32,256]{2,1,0:T(8,128)(2,1)}), bf16[128,32,256]{2,1,0:T(8,128)(2,1)}, u32[]{:S(2)}, u32[]{:S(2)}) async-start(bf16[128,32,256]{2,1,0:T(8,128)(2,1)} %copy.39), calls=%async_computation.1 | async-start | bytes 4194304 | tf_op jit(solution)/shard_map/all_to_all | solution.py:54
  279.3 9.1 %gather_fusion.1 = f32[1024]{0:T(1024)S(1)} fusion(f32[2,2048]{1,0:T(2,128)S(1)} %copy-done.1, s32[1024]{0:T(1024)S(1)} %bitcast.53), kind=kCustom, calls=%fused_computation.1 | custom fusion | bytes 16384 | tf_op jit(solution)/shard_map/jit(take_along_axis)/gather | solution.py:56
  288.5 38.2 %all-to-all-done.1 = bf16[128,32,256]{2,1,0:T(8,128)(2,1)} async-done(((bf16[128,32,256]{2,1,0:T(8,128)(2,1)}), bf16[128,32,256]{2,1,0:T(8,128)(2,1)}, u32[]{:S(2)}, u32[]{:S(2)}) %all-to-all-start.1) | async-done | bytes 2097184 | tf_op jit(solution)/shard_map/all_to_all | solution.py:54
  333.7 119.9 %all-reduce.2.cloned.1.call-done = bf16[2,512,256]{2,1,0:T(8,128)(2,1)} async-done(((bf16[2,512,256]{2,1,0:T(8,128)(2,1)}), bf16[2,512,256]{2,1,0:T(8,128)(2,1)}) %all-reduce.2.cloned.1.call-update) | async-done | bytes 524304 | tf_op jit(solution)/shard_map/psum | solution.py:57
  (199 shorter events, 101.5 us)
Async XLA Ops:
  7.2 253.0 %copy-start = (bf16[1,32,128,128]{3,2,1,0:T(8,128)(2,1)S(1)}, bf16[1,32,128,128]{3,2,1,0:T(8,128)(2,1)}, u32[]{:S(2)}) copy-start(bf16[1,32,128,128]{3,2,1,0:T(8,128)(2,1)} %param.13) | copy-start | bytes 3145732
  164.9 4.0 copy-start.2
  267.8 11.5 %copy-start.1 = (f32[2,2048]{1,0:T(2,128)S(1)}, f32[2,2048]{1,0:T(2,128)}, u32[]{:S(2)}) copy-start(f32[2,2048]{1,0:T(2,128)} %param.9) | copy-start | bytes 49156
  267.8 58.8 %all-to-all-start.1 = ((bf16[128,32,256]{2,1,0:T(8,128)(2,1)}), bf16[128,32,256]{2,1,0:T(8,128)(2,1)}, u32[]{:S(2)}, u32[]{:S(2)}) async-start(bf16[128,32,256]{2,1,0:T(8,128)(2,1)} %copy.39), calls=%async_computation.1 | async-start | bytes 4194304 | tf_op jit(solution)/shard_map/all_to_all | solution.py:54
  279.1 174.6 %all-reduce.2.cloned.1.call-start = ((), (), s32[]{:S(2)}) async-start(), calls=%async_computation.2 | async-start | bytes 1048576 | tf_op jit(solution)/shard_map/psum | solution.py:57
  326.7 2.8 copy-start.3
  332.1 122.9 %copy-start.4 = (s32[2,512]{1,0:T(2,128)S(1)}, s32[2,512]{1,0:T(2,128)}, u32[]{:S(2)}) copy-start(s32[2,512]{1,0:T(2,128)} %param.10) | copy-start | bytes 12292
Sparse Core Ops, SparseCore 0:
  332.2 121.4 all-reduce.1
where the time goes:
time: 466 us; the launch traced here: 465 us
  waiting for transfers between devices  158 us (34%)
  other arithmetic  121 us (26%)
  local copies, waits for them, and re-layouts  75.5 us (16%)
  blocking collectives  72.2 us (15%)
  between operations  14.2 us (3%)
  starting transfers between devices  11.5 us (2%)
  matrix products  11.2 us (2%)
    psum x1, waiting for transfers between devices, local(): summed = lax.psum(gradient.astype(jnp.bfloat16), 'rep').astype(jnp.float32)  120 us
    reduce_sum x32, other arithmetic, counts_block(): return jnp.sum(hits.astype(jnp.int32), axis=-2).astype(jnp.bfloat16)  91.4 us
    all_to_all x1, blocking collectives, local(): lax.all_to_all(pooled, 'shard', split_axis=1, concat_axis=0, tiled=True)  72.2 us
    all_to_all x1, waiting for transfers between devices, local(): lax.all_to_all(dpool, 'shard', split_axis=0, concat_axis=1, tiled=True)  38.2 us
    lt x32, local copies, waits for them, and re-layouts, counts_block(): jnp.arange(slot_rows.shape[-1], dtype=jnp.int32) < length_rows[..., None]  22.2 us
    dynamic_update_slice x32, other arithmetic, local(): lax.map(block_counts, (slot_here.reshape(tab_count * block_count, block_r...  21.7 us
    convert_element_type x1, local copies, waits for them, and re-layouts, local(): pooled = jnp.einsum('tbk,tkd->tbd', counts, rows_low, preferred_element_t...  12.8 us
    gather x1, local copies, waits for them, and re-layouts, local(): table_rows = jnp.take_along_axis(emb_table, touched[:, :, None], axis=1)  12.6 us
  transfers between devices with their start and end apart: 2, of which 2 were waited for; matrix products, arithmetic and copies ran while one was open for 2% of the time, Pallas kernels for 0%

commit v1 on v0

v1 whole, which is shorter than its diff:
```python
import functools

import jax
import jax.numpy as jnp
from jax import lax
from jax.experimental import pallas as pl
from jax.experimental.pallas import tpu as pltpu
from jax.sharding import PartitionSpec as P

MESH = pl.DeviceIdType.MESH
VMEM = pl.BlockSpec(memory_space=pltpu.VMEM)
learn_rate = 0.5
epsilon = 1e-08
LANES = 128
SUB = 16
CORES = 2


def gather_kernel(touched, acc, table, rows, acc_rows):
    t = pl.program_id(0)

    def eight(i, carry):
        for u in range(8):
            k = i * 8 + u
            idx = touched[t, k]
            rows[0, pl.ds(k, 1), :] = table[0, pl.ds(idx, 1), :]
            acc_rows[0, pl.ds(k, 1), :] = jnp.full((1, LANES), acc[t, idx], jnp.float32)
        return carry

    lax.fori_loop(0, touched.shape[1] // 8, eight, 0)


def gather_rows(emb_table, accumulated, touched):
    tabs, size, dim = emb_table.shape
    width = touched.shape[1]
    return pl.pallas_call(
        gather_kernel,
        grid=(tabs,),
        out_shape=(
            jax.ShapeDtypeStruct((tabs, width, dim), jnp.float32),
            jax.ShapeDtypeStruct((tabs, width, LANES), jnp.float32),
        ),
        in_specs=[
            pl.BlockSpec(memory_space=pltpu.SMEM),
            pl.BlockSpec(memory_space=pltpu.SMEM),
            pl.BlockSpec((1, size, dim), lambda t: (t, 0, 0)),
        ],
        out_specs=(
            pl.BlockSpec((1, width, dim), lambda t: (t, 0, 0)),
            pl.BlockSpec((1, width, LANES), lambda t: (t, 0, 0)),
        ),
        compiler_params=pltpu.CompilerParams(vmem_limit_bytes=32 << 20),
    )(touched, accumulated, emb_table)


def main_kernel(
    n_shard, n_rep, n_chunk,
    rows_ref, acc_ref, slot_ref, len_ref, cot_ref,
    inter_ref, new_ref,
    low, counts, pooled, got, mine, dmine, dsend, dgot,
    partial, part_low, half_got, half_low, y_got, sums, other,
    f_send, f_recv, f_own, b_send, b_recv, b_own,
    c_send, c_recv, y_send, y_recv, g_send, g_recv, h_send, h_recv,
):
    me = lax.axis_index("shard")
    rep = lax.axis_index("rep")
    core = lax.rem(rep, CORES)
    y = rep // CORES
    n_y = n_rep // CORES
    tabs, width, dim = rows_ref.shape
    batch = slot_ref.shape[2]
    own = batch // n_shard
    part = own // n_chunk
    n_tab = tabs * n_shard
    blocks = batch // LANES
    per_block = LANES // own
    groups = n_tab // SUB
    per_group = SUB // tabs
    sibling = rep + 1 - 2 * core

    barrier = pltpu.get_barrier_semaphore()

    def greet(i, carry):
        pl.semaphore_signal(
            barrier, inc=1, device_id={"shard": lax.rem(me + i, n_shard)}, device_id_type=MESH
        )
        return carry

    lax.fori_loop(1, n_shard, greet, 0)

    def greet_y(i, carry):
        peer = lax.rem(y + i, n_y) * CORES + core
        pl.semaphore_signal(barrier, inc=1, device_id={"rep": peer}, device_id_type=MESH)
        return carry

    lax.fori_loop(1, n_y, greet_y, 0)
    pl.semaphore_signal(barrier, inc=1, device_id={"rep": sibling}, device_id_type=MESH)

    low[...] = rows_ref[...].astype(jnp.bfloat16)
    pl.semaphore_wait(barrier, n_shard - 1 + n_y - 1 + 1)

    key0 = lax.broadcasted_iota(jnp.int32, (SUB, LANES), 0)
    one = jnp.ones((SUB, LANES), jnp.bfloat16)
    zero = jnp.zeros((SUB, LANES), jnp.bfloat16)

    def start_forward(c, dest):
        src = pooled.at[:, pl.ds(dest * own + c * part, part), :]

        @pl.when(dest == me)
        def _():
            pltpu.make_async_copy(
                src, got.at[pl.ds(me * tabs, tabs), pl.ds(c * part, part), :], f_own.at[c]
            ).start()

        @pl.when(dest != me)
        def _():
            pltpu.make_async_remote_copy(
                src_ref=src,
                dst_ref=got.at[pl.ds(me * tabs, tabs), pl.ds(c * part, part), :],
                send_sem=f_send.at[c],
                recv_sem=f_recv.at[c],
                device_id={"shard": dest},
                device_id_type=MESH,
            ).start()

    def block_of(i):
        away = lax.rem(i, 2) * ((i + 1) // 2) + (1 - lax.rem(i, 2)) * (blocks - i // 2)
        return lax.rem(me // per_block + away, blocks)

    def forward(i, carry):
        block = block_of(i)
        first = pl.multiple_of(block * LANES, LANES)
        for t in range(tabs):
            slots = slot_ref[t, :, pl.ds(first, LANES)]
            sizes = len_ref[t, :, pl.ds(first, LANES)]
            place = lax.broadcasted_iota(jnp.int32, slots.shape, 0)
            slots = jnp.where(place < sizes, slots, -1)
            wide = [
                jnp.broadcast_to(slots[l : l + 1], (SUB, LANES)).astype(jnp.int16)
                for l in range(slots.shape[0])
            ]
            for tile in range(width // SUB):
                key = (key0 + tile * SUB).astype(jnp.int16)
                terms = [jnp.where(key == w, one, zero) for w in wide]
                while len(terms) > 1:
                    terms = [a + b for a, b in zip(terms[::2], terms[1::2])]
                counts[t, pl.ds(tile * SUB, SUB), pl.ds(first, LANES)] = terms[0]
            block_counts = counts[t, :, pl.ds(first, LANES)]
            pooled[t, pl.ds(first, LANES), :] = lax.dot_general(
                block_counts, low[t], (((0,), (0,)), ((), ())), preferred_element_type=jnp.float32
            ).astype(jnp.bfloat16)
        for q in range(per_block):
            start_forward(0, block * per_block + q)
        return carry

    lax.fori_loop(0, blocks, forward, 0)

    for c in range(1, n_chunk):

        def rest(i, carry, c=c):
            block = block_of(i)
            for q in range(per_block):
                start_forward(c, block * per_block + q)
            return carry

        lax.fori_loop(0, blocks, rest, 0)

    swap_row = lax.broadcasted_iota(jnp.int32, (SUB * SUB, SUB * SUB), 0)
    swap_col = lax.broadcasted_iota(jnp.int32, (SUB * SUB, SUB * SUB), 1)
    swapped = lax.rem(swap_col, SUB) * SUB + swap_col // SUB
    swap = jnp.where(swap_row == swapped, 1.0, 0.0).astype(jnp.bfloat16)

    def swap_tile(tile):
        flat = tile.reshape(SUB * SUB, dim)
        out = jnp.dot(swap, flat, preferred_element_type=jnp.float32).astype(jnp.bfloat16)
        return out.reshape(SUB, SUB, dim)

    def bytes_of_all(ref, c, sem):
        view = ref.at[pl.ds(0, n_tab - tabs), pl.ds(c * part, part), :]
        return pltpu.make_async_copy(view, view, sem)

    for c in range(n_chunk):
        bytes_of_all(got, c, f_recv.at[c]).wait()
        kept = got.at[pl.ds(me * tabs, tabs), pl.ds(c * part, part), :]
        pltpu.make_async_copy(kept, kept, f_own.at[c]).wait()

        def to_samples(g, carry, c=c):
            first = pl.multiple_of(g * SUB, SUB)
            mine[pl.ds(c * part, part), pl.ds(first, SUB), :] = swap_tile(
                got[pl.ds(first, SUB), pl.ds(c * part, part), :]
            )
            return carry

        lax.fori_loop(0, groups, to_samples, 0, unroll=2)

        def sample(i, carry, c=c):
            for u in range(4):
                b = c * part + i * 4 + u
                vectors = mine[b]
                inter_ref[0, b] = lax.dot_general(
                    vectors, vectors, (((1,), (1,)), ((), ())), preferred_element_type=jnp.float32
                ).astype(jnp.bfloat16)
                cot = cot_ref[0, b]
                both = jnp.concatenate([cot, cot.T], axis=1)
                dmine[b] = jnp.dot(
                    both,
                    jnp.concatenate([vectors, vectors], axis=0),
                    preferred_element_type=jnp.float32,
                ).astype(jnp.bfloat16)
            return carry

        lax.fori_loop(0, part // 4, sample, 0)

        def to_tables(i, carry, c=c):
            away = lax.rem(i, 2) * ((i + 1) // 2) + (1 - lax.rem(i, 2)) * (groups - i // 2)
            g = lax.rem(me // per_group + away, groups)
            first = pl.multiple_of(g * SUB, SUB)
            dsend[pl.ds(first, SUB), pl.ds(c * part, part), :] = swap_tile(
                dmine[pl.ds(c * part, part), pl.ds(first, SUB), :]
            )
            for q in range(per_group):
                dest = g * per_group + lax.rem(me + q, per_group)
                src = dsend.at[pl.ds(dest * tabs, tabs), pl.ds(c * part, part), :]
                dst = dgot.at[:, pl.ds(me * own + c * part, part), :]

                @pl.when(dest == me)
                def _():
                    pltpu.make_async_copy(src, dst, b_own.at[c]).start()

                @pl.when(dest != me)
                def _():
                    pltpu.make_async_remote_copy(
                        src_ref=src,
                        dst_ref=dst,
                        send_sem=b_send.at[c],
                        recv_sem=b_recv.at[c],
                        device_id={"shard": dest},
                        device_id_type=MESH,
                    ).start()

            return carry

        lax.fori_loop(0, groups, to_tables, 0)

    for c in range(n_chunk):
        bytes_of_all(got, c, b_recv.at[c]).wait()
        kept = got.at[pl.ds(me * tabs, tabs), pl.ds(c * part, part), :]
        pltpu.make_async_copy(kept, kept, b_own.at[c]).wait()

    for t in range(tabs):

        def grad(i, carry, t=t):
            first = pl.multiple_of(i * 256, 256)
            value = jnp.dot(
                counts[t, pl.ds(first, 256), :], dgot[t], preferred_element_type=jnp.float32
            )
            partial[t, pl.ds(first, 256), :] = value
            part_low[t, pl.ds(first, 256), :] = value.astype(jnp.bfloat16)
            return carry

        lax.fori_loop(0, width // 256, grad, 0)

    half = pltpu.make_async_remote_copy(
        src_ref=part_low.at[1 - core],
        dst_ref=half_got,
        send_sem=c_send,
        recv_sem=c_recv,
        device_id={"rep": sibling},
        device_id_type=MESH,
    )
    half.start()
    half.wait()
    total = partial[core] + half_got[...].astype(jnp.float32)
    partial[core] = total
    half_low[...] = total.astype(jnp.bfloat16)

    piece = width // n_y

    def scatter(i, carry):
        peer = lax.rem(y + i, n_y)
        pltpu.make_async_remote_copy(
            src_ref=half_low.at[pl.ds(pl.multiple_of(peer * piece, piece), piece), :],
            dst_ref=y_got.at[y],
            send_sem=y_send,
            recv_sem=y_recv,
            device_id={"rep": peer * CORES + core},
            device_id_type=MESH,
        ).start()
        return carry

    lax.fori_loop(1, n_y, scatter, 0)
    y_got[y] = jnp.zeros((piece, dim), jnp.bfloat16)
    seven = y_got.at[pl.ds(0, n_y - 1)]
    pltpu.make_async_copy(seven, seven, y_recv).wait()
    here = pl.ds(pl.multiple_of(y * piece, piece), piece)
    total = partial[core, here, :]
    for i in range(n_y):
        total = total + y_got[i].astype(jnp.float32)
    sums[core, here, :] = total.astype(jnp.bfloat16)

    def spread(i, carry):
        peer = lax.rem(y + i, n_y)
        pltpu.make_async_remote_copy(
            src_ref=sums.at[core, here, :],
            dst_ref=sums.at[core, here, :],
            send_sem=g_send,
            recv_sem=g_recv,
            device_id={"rep": peer * CORES + core},
            device_id_type=MESH,
        ).start()
        return carry

    lax.fori_loop(1, n_y, spread, 0)
    pltpu.make_async_copy(seven, seven, g_recv).wait()
    last = pltpu.make_async_remote_copy(
        src_ref=sums.at[core],
        dst_ref=other,
        send_sem=h_send,
        recv_sem=h_recv,
        device_id={"rep": sibling},
        device_id_type=MESH,
    )
    last.start()

    def update(t, gradient):
        mean = jnp.sum(gradient * gradient, axis=1, keepdims=True) * (1.0 / dim)
        acc_new = acc_ref[t][:, :1] + mean
        new_ref[t] = rows_ref[t] - learn_rate * gradient / (jnp.sqrt(acc_new) + epsilon)

    update(core, sums[core].astype(jnp.float32))
    last.wait()
    update(1 - core, other[...].astype(jnp.float32))

    for c in range(n_chunk):
        bytes_of_all(got, c, f_send.at[c]).wait()
        bytes_of_all(got, c, b_send.at[c]).wait()
    pltpu.make_async_copy(seven, seven, y_send).wait()
    pltpu.make_async_copy(seven, seven, g_send).wait()


def local(n_shard, n_rep, emb_table, accumulated, touched, bag_slots, lengths, cotangent):
    tabs, width = touched.shape
    dim = emb_table.shape[2]
    batch = bag_slots.shape[2]
    own = batch // n_shard
    n_tab = tabs * n_shard
    n_chunk = own // SUB
    n_y = n_rep // CORES
    rows, acc_rows = gather_rows(emb_table, accumulated, touched)
    slots = jnp.swapaxes(bag_slots[:, 0], 1, 2)
    dma = pltpu.SemaphoreType.DMA
    low = jnp.bfloat16
    return pl.pallas_call(
        functools.partial(main_kernel, n_shard, n_rep, n_chunk),
        out_shape=(
            jax.ShapeDtypeStruct((1, own, n_tab, n_tab), low),
            jax.ShapeDtypeStruct((tabs, width, dim), jnp.float32),
        ),
        in_specs=[VMEM] * 5,
        out_specs=(VMEM, VMEM),
        scratch_shapes=[
            pltpu.VMEM((tabs, width, dim), low),
            pltpu.VMEM((tabs, width, batch), low),
            pltpu.VMEM((tabs, batch, dim), low),
            pltpu.VMEM((n_tab, own, dim), low),
            pltpu.VMEM((own, n_tab, dim), low),
            pltpu.VMEM((own, n_tab, dim), low),
            pltpu.VMEM((n_tab, own, dim), low),
            pltpu.VMEM((tabs, batch, dim), low),
            pltpu.VMEM((tabs, width, dim), jnp.float32),
            pltpu.VMEM((tabs, width, dim), low),
            pltpu.VMEM((width, dim), low),
            pltpu.VMEM((width, dim), low),
            pltpu.VMEM((n_y, width // n_y, dim), low),
            pltpu.VMEM((tabs, width, dim), low),
            pltpu.VMEM((width, dim), low),
            *[dma((n_chunk,))] * 6,
            *[dma] * 8,
        ],
        compiler_params=pltpu.CompilerParams(
            collective_id=0, has_side_effects=True, vmem_limit_bytes=52 << 20
        ),
    )(rows, acc_rows, slots, lengths, cotangent)


def solution(mesh):
    return jax.shard_map(
        functools.partial(local, mesh.shape["shard"], mesh.shape["rep"]),
        mesh=mesh,
        in_specs=(
            P("shard", None, None),
            P("shard", None),
            P("shard", None),
            P("shard", "rep", None, None),
            P("shard", "rep", None),
            P("rep", "shard", None, None),
        ),
        out_specs=(P("rep", "shard", None, None), P("shard", None, None)),
        check_vma=False,
    )
```

time: 466 us -> 194 us (0.42)
  the two profiles are of different devices: /device:TPU:1 before, /device:TPU:335 now
where the time goes in v1:
time: 194 us
  Pallas kernels  186 us (96%)
  local copies, waits for them, and re-layouts  7.79 us (4%)
    pallas_call x1, Pallas kernels, local(): pl.pallas_call(functools.partial(main_kernel, n_shard, n_rep, n_chunk), o...  177 us
    pallas_call x1, Pallas kernels, gather_rows(): pl.pallas_call(gather_kernel, grid=(tabs,), out_shape=(jax.ShapeDtypeStru...  8.8 us
    unnamed x14, local copies, waits for them, and re-layouts  7.79 us

profile of v1, /device:TPU:335, one launch (start us, length us, event | category | flops | bytes accessed | tf_op | source)
XLA Modules:
  0.0 194.1 jit_solution(850753487442672742)
XLA Ops:
  0.6 0.0 copy-start
  0.6 2.2 %copy-done = f32[2,2048,256]{2,1,0:T(8,128)S(1)} copy-done((f32[2,2048,256]{2,1,0:T(8,128)S(1)}, f32[2,2048,256]{2,1,0:T(8,128)}, u32[]{:S(2)}) %copy-start) | copy-done | bytes 4194328
  2.8 0.0 copy-start.3
  2.8 0.7 copy-done.3
  3.5 0.0 copy-start.5
  3.5 0.7 copy-done.5
  4.2 0.0 copy-start.2
  4.2 0.0 copy-start.4
  4.2 8.8 %shard_map.77 = (f32[2,512,256]{2,1,0:T(8,128)S(1)}, f32[2,512,128]{2,1,0:T(8,128)S(1)}) custom-call(s32[2,512]{1,0:T(2,128)S(1)} %copy-done.5, f32[2,2048]{1,0:T(2,128)S(1)} %copy-done.3, f32[2,2048,256]{2,1,0:T(8,128)S(1)} %copy-done), custom_call_target="tpu_custom_call" | custom-call | tf_op jit(solution)/shard_map/pallas_call | solution.py:36
  13.0 0.0 copy-start.1
  13.0 1.0 copy-done.1
  14.0 0.0 copy-done.2
  14.0 0.0 copy-done.4
  14.0 176.8 %shard_map.78 = (bf16[1,32,128,128]{3,2,1,0:T(8,128)(2,1)S(1)}, f32[2,512,256]{2,1,0:T(8,128)}) custom-call(f32[2,512,256]{2,1,0:T(8,128)} %copy-done.1, f32[2,512,128]{2,1,0:T(8,128)S(1)} %get-tuple-element.5.acc_ref, s32[2,16,2048]{2,1,0:T(8,128)S(1)} %bitcast.3, s32[2,1,2048]{2,1,0:T(1,128)S(1)} %copy-done.4, bf16[1,32,128,128]{3,2,1,0:T(8,128)(2,1)} %cot_ref.1), custom_call_target="tpu_custom_call" | custom-call | tf_op jit(solution)/shard_map/pallas_call | solution.py:353
  190.8 1.0 copy.10
  191.8 2.3 %copy.11 = f32[2,512,256]{2,1,0:T(8,128)} copy(f32[2,512,256]{2,1,0:T(8,128)} %get-tuple-element.9) | data formatting | bytes 2097152
Async XLA Ops:
  0.6 2.2 %copy-start = (f32[2,2048,256]{2,1,0:T(8,128)S(1)}, f32[2,2048,256]{2,1,0:T(8,128)}, u32[]{:S(2)}) copy-start(f32[2,2048,256]{2,1,0:T(8,128)} %table.1) | copy-start | bytes 12582916
  2.8 0.7 copy-start.3
  3.5 0.7 copy-start.5
  4.2 9.8 %copy-start.2 = (s32[2,1,2048,16]{2,3,1,0:T(8,128)S(1)}, s32[2,1,2048,16]{2,3,1,0:T(8,128)}, u32[]{:S(2)}) copy-start(s32[2,1,2048,16]{2,3,1,0:T(8,128)} %param.9) | copy-start | bytes 786436
  4.2 9.8 %copy-start.4 = (s32[2,1,2048]{2,1,0:T(1,128)S(1)}, s32[2,1,2048]{2,1,0:T(1,128)}, u32[]{:S(2)}) copy-start(s32[2,1,2048]{2,1,0:T(1,128)} %len_ref.1) | copy-start | bytes 49156
  13.0 1.0 copy-start.1

commit v2 on v0

v2 whole, which is shorter than its diff:
```python
import functools

import jax
import jax.numpy as jnp
from jax import lax
from jax.experimental import pallas as pl
from jax.experimental.pallas import tpu as pltpu
from jax.sharding import PartitionSpec as P

MESH = pl.DeviceIdType.MESH
VMEM = pl.BlockSpec(memory_space=pltpu.VMEM)
HBM = pl.BlockSpec(memory_space=pl.ANY)
learn_rate = 0.5
epsilon = 1e-08
LANES = 128
SUB = 16
CORES = 2


def main_kernel(
    n_shard, n_rep, ring, n_chunk,
    table_ref, acc_ref, touched_ref, slot_ref, len_ref, cot_ref,
    inter_ref, new_ref,
    table, acc, touched, slots, cot, inter, rows, acc_rows, low, counts, pooled, got, mine, dmine, dsend, dgot,
    partial, part_low, half_got, half_low, y_got, sums, new,
    in_sem, out_sem, f_send, f_recv, f_own, b_send, b_recv, b_own,
    c_send, c_recv, y_send, y_recv, g_send, g_recv, h_send, h_recv,
):
    me = lax.axis_index("shard")
    rep = lax.axis_index("rep")
    core = lax.rem(rep, CORES)
    y = rep // CORES
    z = me // ring
    x = lax.rem(me, ring)
    n_y = n_rep // CORES
    n_z = n_shard // ring
    tabs, width, dim = rows.shape
    batch = slot_ref.shape[2]
    deep = slot_ref.shape[1]
    own = batch // n_shard
    span = batch // n_chunk
    n_tab = tabs * n_shard
    sibling = rep + 1 - 2 * core

    loads = [
        pltpu.make_async_copy(touched_ref, touched, in_sem.at[0]),
        pltpu.make_async_copy(acc_ref, acc, in_sem.at[1]),
        *[pltpu.make_async_copy(table_ref.at[t], table.at[t], in_sem.at[2 + t]) for t in range(tabs)],
        pltpu.make_async_copy(cot_ref.at[0], cot, in_sem.at[2 + tabs]),
    ]
    for load in loads:
        load.start()

    barrier = pltpu.get_barrier_semaphore()

    def greet(i, carry):
        pl.semaphore_signal(
            barrier, inc=1, device_id={"shard": lax.rem(me + i, n_shard)}, device_id_type=MESH
        )
        return carry

    lax.fori_loop(1, n_shard, greet, 0)

    def greet_y(i, carry):
        peer = lax.rem(y + i, n_y) * CORES + core
        pl.semaphore_signal(barrier, inc=1, device_id={"rep": peer}, device_id_type=MESH)
        return carry

    lax.fori_loop(1, n_y, greet_y, 0)
    pl.semaphore_signal(barrier, inc=1, device_id={"rep": sibling}, device_id_type=MESH)

    wide = own * ring
    line = wide // n_chunk
    from_lane = lax.broadcasted_iota(jnp.int32, (wide, wide), 0)
    to_lane = lax.broadcasted_iota(jnp.int32, (wide, wide), 1)
    home = lax.rem(to_lane, line) // SUB * own + to_lane // line * SUB + lax.rem(to_lane, SUB)
    sort = jnp.where(from_lane == home, 1.0, 0.0).astype(jnp.bfloat16)

    def sort_slots(r, carry):
        first = pl.multiple_of(r * wide, wide)
        halves = []
        for t in range(tabs):
            ids = slot_ref[t, :, pl.ds(first, wide)]
            sizes = len_ref[t, :, pl.ds(first, wide)]
            place = lax.broadcasted_iota(jnp.int32, ids.shape, 0)
            ids = jnp.where(place < sizes, ids, -1)
            halves += [ids & 255, ids >> 8]
        stack = jnp.concatenate(halves, axis=0).astype(jnp.float32).astype(jnp.bfloat16)
        moved = jnp.dot(stack, sort, preferred_element_type=jnp.float32)
        for t in range(tabs):
            lo = moved[2 * t * deep : (2 * t + 1) * deep]
            hi = moved[(2 * t + 1) * deep : (2 * t + 2) * deep]
            ids = (lo + 256.0 * hi).astype(jnp.int32)
            for c in range(n_chunk):
                slots[t, :, pl.ds(pl.multiple_of(c * span + r * line, line), line)] = ids[
                    :, c * line : (c + 1) * line
                ]
        return carry

    lax.fori_loop(0, n_z, sort_slots, 0)

    key0 = lax.broadcasted_iota(jnp.int32, (SUB, LANES), 0)
    one = jnp.ones((SUB, LANES), jnp.bfloat16)
    zero = jnp.zeros((SUB, LANES), jnp.bfloat16)

    def count(t, first):
        ids = slots[t, :, pl.ds(first, LANES)]
        each = [
            jnp.broadcast_to(ids[l : l + 1], (SUB, LANES)).astype(jnp.int16) for l in range(deep)
        ]
        for tile in range(width // SUB):
            key = (key0 + tile * SUB).astype(jnp.int16)
            terms = [jnp.where(key == e, one, zero) for e in each]
            while len(terms) > 1:
                terms = [a + b for a, b in zip(terms[::2], terms[1::2])]
            counts[t, pl.ds(tile * SUB, SUB), pl.ds(first, LANES)] = terms[0]

    def pool(t, first):
        pooled[t, pl.ds(first, LANES), :] = lax.dot_general(
            counts[t, :, pl.ds(first, LANES)],
            low[t],
            (((0,), (0,)), ((), ())),
            preferred_element_type=jnp.float32,
        ).astype(jnp.bfloat16)

    for load in (loads[0], *loads[2 : 2 + tabs]):
        load.wait()
    gathered = width // n_z

    def count_and_gather(r, carry):
        for t in range(tabs):
            for g in range(gathered // SUB):
                base = pl.multiple_of(r * gathered + g * SUB, SUB)
                picked = jnp.concatenate(
                    [
                        table[t, pl.ds(touched[t, r * gathered + g * SUB + u], 1), :]
                        for u in range(SUB)
                    ],
                    axis=0,
                )
                rows[t, pl.ds(base, SUB), :] = picked
                low[t, pl.ds(base, SUB), :] = picked.astype(jnp.bfloat16)
            count(t, pl.multiple_of(r * line, line))
        return carry

    lax.fori_loop(0, n_z, count_and_gather, 0)
    pl.semaphore_wait(barrier, n_shard - 1 + n_y - 1 + 1)

    def z_pair(i):
        away = lax.rem(i, 2) * ((i + 1) // 2) + (1 - lax.rem(i, 2)) * (n_z - i // 2)
        near = lax.rem(z + away, n_z)
        return near, lax.rem(near + n_z // 2, n_z)

    def send(src, dst, dest, sent, landed, kept):
        @pl.when(dest == me)
        def _():
            pltpu.make_async_copy(src, dst, kept).start()

        @pl.when(dest != me)
        def _():
            pltpu.make_async_remote_copy(
                src_ref=src,
                dst_ref=dst,
                send_sem=sent,
                recv_sem=landed,
                device_id={"shard": dest},
                device_id_type=MESH,
            ).start()

    def forward(i, carry, c):
        pair = z_pair(i)
        for r in pair:
            first = pl.multiple_of(c * span + r * line, line)
            for t in range(tabs):
                if c > 0:
                    count(t, first)
                pool(t, first)

        def out(q, carry):
            for r, column in zip(pair, (lax.rem(x + q, ring), lax.rem(x + ring - q, ring))):
                dest = r * ring + column
                send(
                    pooled.at[:, pl.ds(c * span + dest * SUB, SUB), :],
                    got.at[pl.ds(me * tabs, tabs), pl.ds(c * SUB, SUB), :],
                    dest,
                    f_send.at[c],
                    f_recv.at[c],
                    f_own.at[c],
                )
            return carry

        return lax.fori_loop(0, ring, out, carry)

    for c in range(n_chunk):
        lax.fori_loop(0, n_z // 2, functools.partial(forward, c=c), 0)

    loads[1].wait()

    def gather_acc(i, carry):
        for t in range(tabs):
            base = pl.multiple_of(i * 8, 8)
            acc_rows[t, pl.ds(base, 8), :] = jnp.concatenate(
                [
                    jnp.full((1, LANES), acc[t, touched[t, i * 8 + u]], jnp.float32)
                    for u in range(8)
                ],
                axis=0,
            )
        return carry

    lax.fori_loop(0, width // 8, gather_acc, 0)
    loads[2 + tabs].wait()

    swap_row = lax.broadcasted_iota(jnp.int32, (SUB * SUB, SUB * SUB), 0)
    swap_col = lax.broadcasted_iota(jnp.int32, (SUB * SUB, SUB * SUB), 1)
    swapped = lax.rem(swap_col, SUB) * SUB + swap_col // SUB
    swap = jnp.where(swap_row == swapped, 1.0, 0.0).astype(jnp.bfloat16)

    def swap_tile(tile):
        flat = tile.reshape(SUB * SUB, dim)
        out = jnp.dot(swap, flat, preferred_element_type=jnp.float32).astype(jnp.bfloat16)
        return out.reshape(SUB, SUB, dim)

    def all_of(ref, t0, count_t, sem):
        view = ref.at[pl.ds(t0, count_t), pl.ds(0, (n_shard - 1) * SUB), :]
        return pltpu.make_async_copy(view, view, sem)

    def own_of(t0, count_t, sem):
        view = pooled.at[pl.ds(t0, count_t), pl.ds(0, SUB), :]
        return pltpu.make_async_copy(view, view, sem)

    per_group = SUB // tabs
    for c in range(n_chunk):
        all_of(pooled, 0, tabs, f_recv.at[c]).wait()
        own_of(0, tabs, f_own.at[c]).wait()
        part = pl.ds(c * SUB, SUB)

        def to_samples(g, carry, part=part):
            first = pl.multiple_of(g * SUB, SUB)
            mine[part, pl.ds(first, SUB), :] = swap_tile(got[pl.ds(first, SUB), part, :])
            return carry

        lax.fori_loop(0, n_tab // SUB, to_samples, 0, unroll=2)

        def sample(i, carry, c=c):
            for u in range(4):
                b = c * SUB + i * 4 + u
                vectors = mine[b]
                inter[b] = lax.dot_general(
                    vectors, vectors, (((1,), (1,)), ((), ())), preferred_element_type=jnp.float32
                ).astype(jnp.bfloat16)
                both = jnp.concatenate([cot[b], cot[b].T], axis=1)
                dmine[b] = jnp.dot(
                    both,
                    jnp.concatenate([vectors, vectors], axis=0),
                    preferred_element_type=jnp.float32,
                ).astype(jnp.bfloat16)
            return carry

        lax.fori_loop(0, SUB // 4, sample, 0)
        pltpu.make_async_copy(inter.at[part], inter_ref.at[0, part], out_sem.at[c]).start()

        split = [(0, tabs)] if c < n_chunk - 1 else [(t, 1) for t in range(tabs)]

        def to_tables(i, carry, part=part):
            for g in z_pair(i):
                first = pl.multiple_of(g * SUB, SUB)
                dsend[pl.ds(first, SUB), part, :] = swap_tile(dmine[part, pl.ds(first, SUB), :])
            return carry

        def backward(i, carry, c, k, t0, count_t):
            def out(q, carry):
                columns = (lax.rem(x + q, ring), lax.rem(x + ring - q, ring))
                for r, column in zip(z_pair(i), columns):
                    dest = r * ring + column
                    send(
                        dsend.at[pl.ds(dest * tabs + t0, count_t), pl.ds(c * SUB, SUB), :],
                        dgot.at[pl.ds(t0, count_t), pl.ds(c * span + me * SUB, SUB), :],
                        dest,
                        b_send.at[k],
                        b_recv.at[k],
                        b_own.at[k],
                    )
                return carry

            return lax.fori_loop(0, ring, out, carry)

        for j, (t0, count_t) in enumerate(split):

            def turn(i, carry, c=c, j=j, t0=t0, count_t=count_t):
                if j == 0:
                    to_tables(i, carry)
                return backward(i, carry, c, c + j, t0, count_t)

            lax.fori_loop(0, n_z // 2, turn, 0)

    def gradient(t, c):
        def rows_of(i, carry):
            first = pl.multiple_of(i * 256, 256)
            value = jnp.dot(
                counts[t, pl.ds(first, 256), pl.ds(c * span, span)],
                dgot[t, pl.ds(c * span, span), :],
                preferred_element_type=jnp.float32,
            )
            if c > 0:
                value = value + partial[t, pl.ds(first, 256), :]
            partial[t, pl.ds(first, 256), :] = value
            if c == n_chunk - 1:
                part_low[t, pl.ds(first, 256), :] = value.astype(jnp.bfloat16)
            return carry

        lax.fori_loop(0, width // 256, rows_of, 0)

    for c in range(n_chunk - 1):
        all_of(pooled, 0, tabs, b_recv.at[c]).wait()
        own_of(0, tabs, b_own.at[c]).wait()
        for t in range(tabs):
            gradient(t, c)

    half = width // CORES
    piece = half // n_y
    kept = pl.ds(pl.multiple_of(core * half, half), half)
    given = pl.ds(pl.multiple_of((1 - core) * half, half), half)
    here = pl.ds(pl.multiple_of(core * half + y * piece, piece), piece)
    last = n_chunk - 1
    ends = []
    for t in range(tabs):
        all_of(pooled, t, 1, b_recv.at[last + t]).wait()
        own_of(t, 1, b_own.at[last + t]).wait()
        gradient(t, last)
        trade = pltpu.make_async_remote_copy(
            src_ref=part_low.at[t, given, :],
            dst_ref=half_got.at[t],
            send_sem=c_send.at[t],
            recv_sem=c_recv.at[t],
            device_id={"rep": sibling},
            device_id_type=MESH,
        )
        trade.start()
        trade.wait()
        total = partial[t, kept, :] + half_got[t].astype(jnp.float32)
        partial[t, kept, :] = total
        half_low[t] = total.astype(jnp.bfloat16)

        def scatter(i, carry, t=t):
            peer = lax.rem(y + i, n_y)
            pltpu.make_async_remote_copy(
                src_ref=half_low.at[t, pl.ds(pl.multiple_of(peer * piece, piece), piece), :],
                dst_ref=y_got.at[t, y],
                send_sem=y_send.at[t],
                recv_sem=y_recv.at[t],
                device_id={"rep": peer * CORES + core},
                device_id_type=MESH,
            ).start()
            return carry

        lax.fori_loop(1, n_y, scatter, 0)
        y_got[t, y] = jnp.zeros((piece, dim), jnp.bfloat16)
        others = y_got.at[t, pl.ds(0, n_y - 1)]
        pltpu.make_async_copy(others, others, y_recv.at[t]).wait()
        total = partial[t, here, :]
        for i in range(n_y):
            total = total + y_got[t, i].astype(jnp.float32)
        sums[t, here, :] = total.astype(jnp.bfloat16)

        def spread(i, carry, t=t):
            peer = lax.rem(y + i, n_y)
            pltpu.make_async_remote_copy(
                src_ref=sums.at[t, here, :],
                dst_ref=sums.at[t, here, :],
                send_sem=g_send.at[t],
                recv_sem=g_recv.at[t],
                device_id={"rep": peer * CORES + core},
                device_id_type=MESH,
            ).start()
            return carry

        lax.fori_loop(1, n_y, spread, 0)
        pltpu.make_async_copy(others, others, g_recv.at[t]).wait()
        end = pltpu.make_async_remote_copy(
            src_ref=sums.at[t, kept, :],
            dst_ref=sums.at[t, kept, :],
            send_sem=h_send.at[t],
            recv_sem=h_recv.at[t],
            device_id={"rep": sibling},
            device_id_type=MESH,
        )
        end.start()
        end.wait()
        summed = sums[t].astype(jnp.float32)
        mean = jnp.sum(summed * summed, axis=1, keepdims=True) * (1.0 / dim)
        scale = learn_rate / (jnp.sqrt(acc_rows[t][:, :1] + mean) + epsilon)
        new[t] = rows[t] - summed * scale
        out = pltpu.make_async_copy(new.at[t], new_ref.at[t], out_sem.at[n_chunk + t])
        out.start()
        ends.append(out)

    for c in range(n_chunk):
        all_of(pooled, 0, tabs, f_send.at[c]).wait()
        part = pl.ds(c * SUB, SUB)
        pltpu.make_async_copy(inter.at[part], inter_ref.at[0, part], out_sem.at[c]).wait()
    for c in range(n_chunk - 1):
        all_of(pooled, 0, tabs, b_send.at[c]).wait()
    for t in range(tabs):
        all_of(pooled, t, 1, b_send.at[last + t]).wait()
        others = y_got.at[t, pl.ds(0, n_y - 1)]
        pltpu.make_async_copy(others, others, y_send.at[t]).wait()
        pltpu.make_async_copy(others, others, g_send.at[t]).wait()
        ends[t].wait()


def local(n_shard, n_rep, emb_table, accumulated, touched, bag_slots, lengths, cotangent):
    tabs, width = touched.shape
    size, dim = emb_table.shape[1:]
    batch = bag_slots.shape[2]
    own = batch // n_shard
    n_tab = tabs * n_shard
    n_chunk = own // SUB
    n_y = n_rep // CORES
    ring = SUB // tabs
    half = width // CORES
    slots = jnp.swapaxes(bag_slots[:, 0], 1, 2)
    dma = pltpu.SemaphoreType.DMA
    low = jnp.bfloat16
    f32 = jnp.float32
    return pl.pallas_call(
        functools.partial(main_kernel, n_shard, n_rep, ring, n_chunk),
        out_shape=(
            jax.ShapeDtypeStruct((1, own, n_tab, n_tab), low),
            jax.ShapeDtypeStruct((tabs, width, dim), f32),
        ),
        in_specs=[HBM, HBM, HBM, VMEM, VMEM, HBM],
        out_specs=(HBM, HBM),
        scratch_shapes=[
            pltpu.VMEM((tabs, size, dim), f32),
            pltpu.SMEM((tabs, size), f32),
            pltpu.SMEM((tabs, width), jnp.int32),
            pltpu.VMEM(slots.shape, jnp.int32),
            pltpu.VMEM((own, n_tab, n_tab), low),
            pltpu.VMEM((own, n_tab, n_tab), low),
            pltpu.VMEM((tabs, width, dim), f32),
            pltpu.VMEM((tabs, width, LANES), f32),
            pltpu.VMEM((tabs, width, dim), low),
            pltpu.VMEM((tabs, width, batch), low),
            pltpu.VMEM((tabs, batch, dim), low),
            pltpu.VMEM((n_tab, own, dim), low),
            pltpu.VMEM((own, n_tab, dim), low),
            pltpu.VMEM((own, n_tab, dim), low),
            pltpu.VMEM((n_tab, own, dim), low),
            pltpu.VMEM((tabs, batch, dim), low),
            pltpu.VMEM((tabs, width, dim), f32),
            pltpu.VMEM((tabs, width, dim), low),
            pltpu.VMEM((tabs, half, dim), low),
            pltpu.VMEM((tabs, half, dim), low),
            pltpu.VMEM((tabs, n_y, half // n_y, dim), low),
            pltpu.VMEM((tabs, width, dim), low),
            pltpu.VMEM((tabs, width, dim), f32),
            dma((3 + tabs,)),
            dma((n_chunk + tabs,)),
            *[dma((n_chunk,))] * 3,
            *[dma((n_chunk - 1 + tabs,))] * 3,
            *[dma((tabs,))] * 8,
        ],
        compiler_params=pltpu.CompilerParams(
            collective_id=0, has_side_effects=True, vmem_limit_bytes=56 << 20
        ),
    )(emb_table, accumulated, touched, slots, lengths, cotangent)


def solution(mesh):
    return jax.shard_map(
        functools.partial(local, mesh.shape["shard"], mesh.shape["rep"]),
        mesh=mesh,
        in_specs=(
            P("shard", None, None),
            P("shard", None),
            P("shard", None),
            P("shard", "rep", None, None),
            P("shard", "rep", None),
            P("rep", "shard", None, None),
        ),
        out_specs=(P("rep", "shard", None, None), P("shard", None, None)),
        check_vma=False,
    )
```

time: 466 us -> 177 us (0.38)
  Pallas kernels: 0 us -> 171 us
  waiting for transfers between devices: 158 us -> 0 us
  other arithmetic: 121 us -> 0 us
  blocking collectives: 72.2 us -> 0 us
  local copies, waits for them, and re-layouts: 75.5 us -> 4.57 us
  between operations: 14.2 us -> 0.64 us
  starting transfers between devices: 11.5 us -> 0 us
  matrix products: 11.2 us -> 0 us
    pallas_call x0 -> x1, Pallas kernels: none -> 171 us  [local(): pl.pallas_call(functools.partial(main_kernel, n_shard, n_rep, ring, n_chu...]
    psum x1 -> x0, waiting for transfers between devices: 120 us -> none  [local(): summed = lax.psum(gradient.astype(jnp.bfloat16), 'rep').astype(jnp.float32)]
    reduce_sum x33 -> x0, other arithmetic: 92.6 us -> none  [the longest x32 91.4 us: counts_block(): return jnp.sum(hits.astype(jnp.int32), axis=-2).astype(jnp.bfloat16)]
    all_to_all x1 -> x0, blocking collectives: 72.2 us -> none  [local(): lax.all_to_all(pooled, 'shard', split_axis=1, concat_axis=0, tiled=True)]
    all_to_all x1 -> x0, waiting for transfers between devices: 38.2 us -> none  [local(): lax.all_to_all(dpool, 'shard', split_axis=0, concat_axis=1, tiled=True)]
    lt x32 -> x0, local copies, waits for them, and re-layouts: 22.2 us -> none  [counts_block(): jnp.arange(slot_rows.shape[-1], dtype=jnp.int32) < length_rows[..., None]]
    gather x3 -> x0, local copies, waits for them, and re-layouts: 21.8 us -> none  [the longest x1 12.6 us: local(): table_rows = jnp.take_along_axis(emb_table, touched[:, :, None], axis=1)]
    dynamic_update_slice x32 -> x0, other arithmetic: 21.7 us -> none  [local(): lax.map(block_counts, (slot_here.reshape(tab_count * block_count, block_r...]
  transfers between devices with their start and end apart: 2 -> 0, of which waited for: 2 -> 0; matrix products, arithmetic and copies ran while one was open for 2% -> 0% of each run, Pallas kernels for 0% -> 0%
where the time goes in v2:
time: 177 us; the launch traced here: 176 us
  Pallas kernels  171 us (97%)
  local copies, waits for them, and re-layouts  4.57 us (3%)
    pallas_call x1, Pallas kernels, local(): pl.pallas_call(functools.partial(main_kernel, n_shard, n_rep, ring, n_chu...  171 us
    unnamed x2, local copies, waits for them, and re-layouts  4.57 us

profile of v2, /device:TPU:1, one launch (start us, length us, event | category | flops | bytes accessed | tf_op | source)
XLA Modules:
  0.0 176.3 jit_solution(1654163615675049583)
XLA Ops:
  0.6 171.1 %shard_map.77 = (bf16[1,32,128,128]{3,2,1,0:T(8,128)(2,1)}, f32[2,512,256]{2,1,0:T(8,128)}) custom-call(f32[2,2048,256]{2,1,0:T(8,128)} %table_ref.1, f32[2,2048]{1,0:T(2,128)} %acc_ref.1, s32[2,512]{1,0:T(2,128)} %touched_ref.1, s32[2,16,2048]{2,1,0:T(8,128)} %bitcast.3, s32[2,1,2048]{2,1,0:T(1,128)} %len_ref.1, bf16[1,32,128,128]{3,2,1,0:T(8,128)(2,1)} %cot_ref.1), custom_call_target="tpu_custom_call" | custom-call | tf_op jit(solution)/shard_map/pallas_call | solution.py:426
  171.7 2.3 %copy.10 = bf16[1,32,128,128]{3,2,1,0:T(8,128)(2,1)} copy(bf16[1,32,128,128]{3,2,1,0:T(8,128)(2,1)} %get-tuple-element.4) | data formatting | bytes 2097152
  174.0 2.3 %copy.11 = f32[2,512,256]{2,1,0:T(8,128)} copy(f32[2,512,256]{2,1,0:T(8,128)} %get-tuple-element.5) | data formatting | bytes 2097152

commit v3 on v2

--- a/solution.py
+++ b/solution.py
@@ -23,8 +23,12 @@
     inter_ref, new_ref,
     table, acc, touched, slots, cot, inter, rows, acc_rows, low, counts, pooled, got, mine, dmine, dsend, dgot,
     partial, part_low, half_got, half_low, y_got, sums, new,
+    slots_out, slots_far, low_far, counts_far, pooled_far, dfar,
+    far_low, far_half, far_kept, far_half_low, far_y, far_out, far_in,
     in_sem, out_sem, f_send, f_recv, f_own, b_send, b_recv, b_own,
     c_send, c_recv, y_send, y_recv, g_send, g_recv, h_send, h_recv,
+    e_send, e_recv, e_own, s_send, s_recv, r_send, r_recv, w_send, w_recv, v_send, v_recv,
+    i_send, i_recv, j_send, j_recv, k_send, k_recv,
 ):
     me = lax.axis_index("shard")
     rep = lax.axis_index("rep")
@@ -41,6 +45,12 @@
     span = batch // n_chunk
     n_tab = tabs * n_shard
     sibling = rep + 1 - 2 * core
+    turn = 1 - 2 * core
+    opposite = lax.rem(z + n_z // 2, n_z) * ring + lax.rem(x + ring // 2, ring)
+    near_x = (0, 1, -1, 2)
+    far_x = (4, 5, 3, 6)
+    dgot[...] = jnp.zeros_like(dgot)
+    dfar[...] = jnp.zeros_like(dfar)
 
     loads = [
         pltpu.make_async_copy(touched_ref, touched, in_sem.at[0]),
@@ -92,9 +102,11 @@
             hi = moved[(2 * t + 1) * deep : (2 * t + 2) * deep]
             ids = (lo + 256.0 * hi).astype(jnp.int32)
             for c in range(n_chunk):
-                slots[t, :, pl.ds(pl.multiple_of(c * span + r * line, line), line)] = ids[
-                    :, c * line : (c + 1) * line
-                ]
+                lanes = pl.ds(pl.multiple_of(c * span + r * line, line), line)
+                slots[t, :, lanes] = ids[:, c * line : (c + 1) * line]
+                slots_out[pl.ds(t * deep, deep), lanes] = ids[:, c * line : (c + 1) * line].astype(
+                    jnp.int16
+                )
         return carry
 
     lax.fori_loop(0, n_z, sort_slots, 0)
@@ -103,8 +115,7 @@
     one = jnp.ones((SUB, LANES), jnp.bfloat16)
     zero = jnp.zeros((SUB, LANES), jnp.bfloat16)
 
-    def count(t, first):
-        ids = slots[t, :, pl.ds(first, LANES)]
+    def count(ids, t, to, first):
         each = [
             jnp.broadcast_to(ids[l : l + 1], (SUB, LANES)).astype(jnp.int16) for l in range(deep)
         ]
@@ -113,12 +124,15 @@
             terms = [jnp.where(key == e, one, zero) for e in each]
             while len(terms) > 1:
                 terms = [a + b for a, b in zip(terms[::2], terms[1::2])]
-            counts[t, pl.ds(tile * SUB, SUB), pl.ds(first, LANES)] = terms[0]
-
-    def pool(t, first):
-        pooled[t, pl.ds(first, LANES), :] = lax.dot_general(
-            counts[t, :, pl.ds(first, LANES)],
-            low[t],
+            to[t, pl.ds(tile * SUB, SUB), pl.ds(first, LANES)] = terms[0]
+
+    def count_own(t, first):
+        count(slots[t, :, pl.ds(first, LANES)], t, counts, first)
+
+    def pool(t, first, made, weights, to):
+        to[t, pl.ds(first, LANES), :] = lax.dot_general(
+            made[t, :, pl.ds(first, LANES)],
+            weights[t],
             (((0,), (0,)), ((), ())),
             preferred_element_type=jnp.float32,
         ).astype(jnp.bfloat16)
@@ -140,16 +154,47 @@
                 )
                 rows[t, pl.ds(base, SUB), :] = picked
                 low[t, pl.ds(base, SUB), :] = picked.astype(jnp.bfloat16)
-            count(t, pl.multiple_of(r * line, line))
+            count_own(t, pl.multiple_of(r * line, line))
         return carry
 
     lax.fori_loop(0, n_z, count_and_gather, 0)
     pl.semaphore_wait(barrier, n_shard - 1 + n_y - 1 + 1)
 
-    def z_pair(i):
+    def z_pair(i, way):
         away = lax.rem(i, 2) * ((i + 1) // 2) + (1 - lax.rem(i, 2)) * (n_z - i // 2)
-        near = lax.rem(z + away, n_z)
+        near = lax.rem(z + way * away + 2 * n_z, n_z)
         return near, lax.rem(near + n_z // 2, n_z)
+
+    def x_at(away, way):
+        return lax.rem(x + way * away + 2 * ring, ring)
+
+    share = width // n_y
+    lent = pl.ds(pl.multiple_of(y * share, share), share)
+    lend_rows = pltpu.make_async_remote_copy(
+        src_ref=low.at[core, lent, :],
+        dst_ref=low_far.at[core, lent, :],
+        send_sem=r_send,
+        recv_sem=r_recv,
+        device_id={"shard": opposite},
+        device_id_type=MESH,
+    )
+    lend_rows.start()
+
+    def lend_slots(i, carry):
+        far = z_pair(i, turn)[1]
+        for c in range(n_chunk):
+            lanes = pl.ds(pl.multiple_of(c * span + far * line, line), line)
+            pltpu.make_async_remote_copy(
+                src_ref=slots_out.at[:, lanes],
+                dst_ref=slots_far.at[:, lanes],
+                send_sem=s_send,
+                recv_sem=s_recv,
+                device_id={"shard": opposite},
+                device_id_type=MESH,
+            ).start()
+        return carry
+
+    lax.fori_loop(0, n_z // 2, lend_slots, 0)
 
     def send(src, dst, dest, sent, landed, kept):
         @pl.when(dest == me)
@@ -168,31 +213,88 @@
             ).start()
 
     def forward(i, carry, c):
-        pair = z_pair(i)
+        pair = z_pair(i, turn)
         for r in pair:
-            first = pl.multiple_of(c * span + r * line, line)
             for t in range(tabs):
-                if c > 0:
-                    count(t, first)
-                pool(t, first)
-
-        def out(q, carry):
-            for r, column in zip(pair, (lax.rem(x + q, ring), lax.rem(x + ring - q, ring))):
-                dest = r * ring + column
-                send(
-                    pooled.at[:, pl.ds(c * span + dest * SUB, SUB), :],
-                    got.at[pl.ds(me * tabs, tabs), pl.ds(c * SUB, SUB), :],
-                    dest,
-                    f_send.at[c],
-                    f_recv.at[c],
-                    f_own.at[c],
-                )
-            return carry
-
-        return lax.fori_loop(0, ring, out, carry)
-
-    for c in range(n_chunk):
-        lax.fori_loop(0, n_z // 2, functools.partial(forward, c=c), 0)
+                pool(t, pl.multiple_of(c * span + r * line, line), counts, low, pooled)
+
+        def out(r, column):
+            dest = r * ring + column
+            send(
+                pooled.at[:, pl.ds(c * span + dest * SUB, SUB), :],
+                got.at[pl.ds(me * tabs, tabs), pl.ds(c * SUB, SUB), :],
+                dest,
+                f_send.at[c],
+                f_recv.at[c],
+                f_own.at[c],
+            )
+
+        for j in range(ring // 2):
+            out(pair[0], x_at(near_x[j], turn))
+            out(pair[1], x_at(-near_x[j], -turn))
+            out(pair[0], x_at(far_x[j], turn))
+        return carry
+
+    def forward_far(i, carry, c):
+        near, far = z_pair(i, turn)
+        first = pl.multiple_of(c * span + far * line, line)
+        for t in range(tabs):
+            ids = slots_far[pl.ds(t * deep, deep), pl.ds(c * span + near * line, line)]
+            ids = pltpu.roll(ids.astype(jnp.int32), line // 2, 1)
+            count(ids, t, counts_far, first)
+            pool(t, first, counts_far, low_far, pooled_far)
+        for j in range(ring // 2):
+            column = x_at(far_x[j], turn)
+            send(
+                pooled_far.at[:, pl.ds(c * span + (far * ring + column) * SUB, SUB), :],
+                got.at[pl.ds(opposite * tabs, tabs), pl.ds(c * SUB, SUB), :],
+                near * ring + lax.rem(column + ring // 2, ring),
+                f_send.at[c],
+                f_recv.at[c],
+                f_own.at[c],
+            )
+        return carry
+
+    def count_later(r, carry, c):
+        for t in range(tabs):
+            count_own(t, pl.multiple_of(c * span + r * line, line))
+        return carry
+
+    lax.fori_loop(0, n_z // 2, functools.partial(forward, c=0), 0)
+    lax.fori_loop(0, n_z // 2, functools.partial(count_later, c=1), 0)
+    lend_rows.wait_recv()
+
+    def lend_y(i, carry):
+        peer = lax.rem(y + i, n_y)
+        pltpu.make_async_remote_copy(
+            src_ref=low_far.at[core, lent, :],
+            dst_ref=low_far.at[core, lent, :],
+            send_sem=w_send,
+            recv_sem=w_recv,
+            device_id={"rep": peer * CORES + core},
+            device_id_type=MESH,
+        ).start()
+        return carry
+
+    lax.fori_loop(1, n_y, lend_y, 0)
+    lax.fori_loop(n_z // 2, n_z, functools.partial(count_later, c=1), 0)
+    shares = low_far.at[0, pl.ds(0, (n_y - 1) * share), :]
+    pltpu.make_async_copy(shares, shares, w_recv).wait()
+    lend_core = pltpu.make_async_remote_copy(
+        src_ref=low_far.at[core],
+        dst_ref=low_far.at[core],
+        send_sem=v_send,
+        recv_sem=v_recv,
+        device_id={"rep": sibling},
+        device_id_type=MESH,
+    )
+    lend_core.start()
+    lines = slots_out.at[:, pl.ds(0, n_chunk * line * (n_z // 2))]
+    pltpu.make_async_copy(lines, lines, s_recv).wait()
+    lend_core.wait_recv()
+    lax.fori_loop(0, n_z // 2, functools.partial(forward_far, c=0), 0)
+    lax.fori_loop(0, n_z // 2, functools.partial(forward, c=1), 0)
+    lax.fori_loop(0, n_z // 2, functools.partial(forward_far, c=1), 0)
 
     loads[1].wait()
 
@@ -221,18 +323,15 @@
         out = jnp.dot(swap, flat, preferred_element_type=jnp.float32).astype(jnp.bfloat16)
         return out.reshape(SUB, SUB, dim)
 
-    def all_of(ref, t0, count_t, sem):
-        view = ref.at[pl.ds(t0, count_t), pl.ds(0, (n_shard - 1) * SUB), :]
+    def bytes_of(devices, t0, count_t, sem):
+        view = pooled.at[pl.ds(t0, count_t), pl.ds(0, devices * SUB), :]
         return pltpu.make_async_copy(view, view, sem)
 
-    def own_of(t0, count_t, sem):
-        view = pooled.at[pl.ds(t0, count_t), pl.ds(0, SUB), :]
-        return pltpu.make_async_copy(view, view, sem)
-
-    per_group = SUB // tabs
+    near_both = (n_z // 2) * (ring // 2)
+    direct = n_shard - near_both
     for c in range(n_chunk):
-        all_of(pooled, 0, tabs, f_recv.at[c]).wait()
-        own_of(0, tabs, f_own.at[c]).wait()
+        bytes_of(n_shard - 2, 0, tabs, f_recv.at[c]).wait()
+        bytes_of(2, 0, tabs, f_own.at[c]).wait()
         part = pl.ds(c * SUB, SUB)
 
         def to_samples(g, carry, part=part):
@@ -262,16 +361,35 @@
 
         split = [(0, tabs)] if c < n_chunk - 1 else [(t, 1) for t in range(tabs)]
 
-        def to_tables(i, carry, part=part):
-            for g in z_pair(i):
-                first = pl.multiple_of(g * SUB, SUB)
-                dsend[pl.ds(first, SUB), part, :] = swap_tile(dmine[part, pl.ds(first, SUB), :])
+        def to_tables(g, carry, part=part):
+            first = pl.multiple_of(g * SUB, SUB)
+            dsend[pl.ds(first, SUB), part, :] = swap_tile(dmine[part, pl.ds(first, SUB), :])
             return carry
 
-        def backward(i, carry, c, k, t0, count_t):
-            def out(q, carry):
-                columns = (lax.rem(x + q, ring), lax.rem(x + ring - q, ring))
-                for r, column in zip(z_pair(i), columns):
+        lax.fori_loop(0, n_tab // SUB, to_tables, 0, unroll=2)
+
+        def backward_far(i, carry, c=c):
+            near, far = z_pair(i, -turn)
+            for j in range(ring // 2):
+                column = x_at(far_x[j], -turn)
+                send(
+                    dsend.at[pl.ds((far * ring + column) * tabs, tabs), pl.ds(c * SUB, SUB), :],
+                    dfar.at[:, pl.ds(c * span + opposite * SUB, SUB), :],
+                    near * ring + lax.rem(column + ring // 2, ring),
+                    e_send.at[c],
+                    e_recv.at[c],
+                    e_own.at[c],
+                )
+            return carry
+
+        lax.fori_loop(0, n_z // 2, backward_far, 0)
+
+        for j, (t0, count_t) in enumerate(split):
+
+            def backward(i, carry, c=c, k=c + j, t0=t0, count_t=count_t):
+                pair = z_pair(i, -turn)
+
+                def out(r, column):
                     dest = r * ring + column
                     send(
                         dsend.at[pl.ds(dest * tabs + t0, count_t), pl.ds(c * SUB, SUB), :],
@@ -281,18 +399,14 @@
                         b_recv.at[k],
                         b_own.at[k],
                     )
+
+                for u in range(ring // 2):
+                    out(pair[0], x_at(near_x[u], -turn))
+                    out(pair[1], x_at(-near_x[u], turn))
+                    out(pair[0], x_at(far_x[u], -turn))
                 return carry
 
-            return lax.fori_loop(0, ring, out, carry)
-
-        for j, (t0, count_t) in enumerate(split):
-
-            def turn(i, carry, c=c, j=j, t0=t0, count_t=count_t):
-                if j == 0:
-                    to_tables(i, carry)
-                return backward(i, carry, c, c + j, t0, count_t)
-
-            lax.fori_loop(0, n_z // 2, turn, 0)
+            lax.fori_loop(0, n_z // 2, backward, 0)
 
     def gradient(t, c):
         def rows_of(i, carry):
@@ -311,24 +425,81 @@
 
         lax.fori_loop(0, width // 256, rows_of, 0)
 
-    for c in range(n_chunk - 1):
-        all_of(pooled, 0, tabs, b_recv.at[c]).wait()
-        own_of(0, tabs, b_own.at[c]).wait()
-        for t in range(tabs):
-            gradient(t, c)
-
     half = width // CORES
     piece = half // n_y
     kept = pl.ds(pl.multiple_of(core * half, half), half)
     given = pl.ds(pl.multiple_of((1 - core) * half, half), half)
     here = pl.ds(pl.multiple_of(core * half + y * piece, piece), piece)
     last = n_chunk - 1
-    ends = []
+
+    for c in range(last):
+        bytes_of(direct - 1, 0, tabs, b_recv.at[c]).wait()
+        bytes_of(1, 0, tabs, b_own.at[c]).wait()
+        for t in range(tabs):
+            gradient(t, c)
+
+    for c in range(n_chunk):
+        bytes_of(near_both - 1, 0, tabs, e_recv.at[c]).wait()
+        bytes_of(1, 0, tabs, e_own.at[c]).wait()
     for t in range(tabs):
-        all_of(pooled, t, 1, b_recv.at[last + t]).wait()
-        own_of(t, 1, b_own.at[last + t]).wait()
-        gradient(t, last)
-        trade = pltpu.make_async_remote_copy(
+        for rows_at in range(0, width, 256):
+            total = jnp.zeros((256, dim), jnp.float32)
+            for i in range(n_z // 2):
+                far = z_pair(i, turn)[1]
+                for c in range(n_chunk):
+                    block = pl.ds(pl.multiple_of(c * span + far * line, line), line)
+                    total = total + jnp.dot(
+                        counts_far[t, rows_at : rows_at + 256, block],
+                        dfar[t, block, :],
+                        preferred_element_type=jnp.float32,
+                    )
+            far_kept[t, rows_at : rows_at + 256, :] = total
+            far_low[t, rows_at : rows_at + 256, :] = total.astype(jnp.bfloat16)
+    far_trade = pltpu.make_async_remote_copy(
+        src_ref=far_low.at[:, given, :],
+        dst_ref=far_half,
+        send_sem=i_send,
+        recv_sem=i_recv,
+        device_id={"rep": sibling},
+        device_id_type=MESH,
+    )
+    far_trade.start()
+    far_trade.wait()
+    total = far_kept[:, kept, :] + far_half[...].astype(jnp.float32)
+    far_half_low[...] = total.astype(jnp.bfloat16)
+
+    def far_scatter(i, carry):
+        peer = lax.rem(y + i, n_y)
+        pltpu.make_async_remote_copy(
+            src_ref=far_half_low.at[:, pl.ds(pl.multiple_of(peer * piece, piece), piece), :],
+            dst_ref=far_y.at[y],
+            send_sem=j_send,
+            recv_sem=j_recv,
+            device_id={"rep": peer * CORES + core},
+            device_id_type=MESH,
+        ).start()
+        return carry
+
+    lax.fori_loop(1, n_y, far_scatter, 0)
+    far_y[y] = far_half_low[:, pl.ds(pl.multiple_of(y * piece, piece), piece), :]
+    far_others = far_y.at[pl.ds(0, n_y - 1)]
+    pltpu.make_async_copy(far_others, far_others, j_recv).wait()
+    total = far_y[0].astype(jnp.float32)
+    for i in range(1, n_y):
+        total = total + far_y[i].astype(jnp.float32)
+    far_out[...] = total.astype(jnp.bfloat16)
+    far_home = pltpu.make_async_remote_copy(
+        src_ref=far_out,
+        dst_ref=far_in,
+        send_sem=k_send,
+        recv_sem=k_recv,
+        device_id={"shard": opposite},
+        device_id_type=MESH,
+    )
+    far_home.start()
+
+    def trade(t):
+        return pltpu.make_async_remote_copy(
             src_ref=part_low.at[t, given, :],
             dst_ref=half_got.at[t],
             send_sem=c_send.at[t],
@@ -336,13 +507,34 @@
             device_id={"rep": sibling},
             device_id_type=MESH,
         )
-        trade.start()
-        trade.wait()
+
+    def finish(t):
+        return pltpu.make_async_remote_copy(
+            src_ref=sums.at[t, kept, :],
+            dst_ref=sums.at[t, kept, :],
+            send_sem=h_send.at[t],
+            recv_sem=h_recv.at[t],
+            device_id={"rep": sibling},
+            device_id_type=MESH,
+        )
+
+    def others(t, sem):
+        view = y_got.at[t, pl.ds(0, n_y - 1)]
+        return pltpu.make_async_copy(view, view, sem)
+
+    def take(t):
+        bytes_of(direct - 1, t, 1, b_recv.at[last + t]).wait()
+        bytes_of(1, t, 1, b_own.at[last + t]).wait()
+        gradient(t, last)
+        trade(t).start()
+
+    def scatter(t):
+        trade(t).wait()
         total = partial[t, kept, :] + half_got[t].astype(jnp.float32)
         partial[t, kept, :] = total
         half_low[t] = total.astype(jnp.bfloat16)
 
-        def scatter(i, carry, t=t):
+        def one_piece(i, carry):
             peer = lax.rem(y + i, n_y)
             pltpu.make_async_remote_copy(
                 src_ref=half_low.at[t, pl.ds(pl.multiple_of(peer * piece, piece), piece), :],
@@ -354,16 +546,17 @@
             ).start()
             return carry
 
-        lax.fori_loop(1, n_y, scatter, 0)
+        lax.fori_loop(1, n_y, one_piece, 0)
         y_got[t, y] = jnp.zeros((piece, dim), jnp.bfloat16)
-        others = y_got.at[t, pl.ds(0, n_y - 1)]
-        pltpu.make_async_copy(others, others, y_recv.at[t]).wait()
-        total = partial[t, here, :]
+
+    def spread(t):
+        others(t, y_recv.at[t]).wait()
+        total = partial[t, here, :] + far_in[t].astype(jnp.float32)
         for i in range(n_y):
             total = total + y_got[t, i].astype(jnp.float32)
         sums[t, here, :] = total.astype(jnp.bfloat16)
 
-        def spread(i, carry, t=t):
+        def one_peer(i, carry):
             peer = lax.rem(y + i, n_y)
             pltpu.make_async_remote_copy(
                 src_ref=sums.at[t, here, :],
@@ -375,38 +568,49 @@
             ).start()
             return carry
 
-        lax.fori_loop(1, n_y, spread, 0)
-        pltpu.make_async_copy(others, others, g_recv.at[t]).wait()
-        end = pltpu.make_async_remote_copy(
-            src_ref=sums.at[t, kept, :],
-            dst_ref=sums.at[t, kept, :],
-            send_sem=h_send.at[t],
-            recv_sem=h_recv.at[t],
-            device_id={"rep": sibling},
-            device_id_type=MESH,
-        )
-        end.start()
-        end.wait()
+        lax.fori_loop(1, n_y, one_peer, 0)
+
+    def swap_halves(t):
+        others(t, g_recv.at[t]).wait()
+        finish(t).start()
+
+    def update(t):
+        finish(t).wait()
         summed = sums[t].astype(jnp.float32)
         mean = jnp.sum(summed * summed, axis=1, keepdims=True) * (1.0 / dim)
         scale = learn_rate / (jnp.sqrt(acc_rows[t][:, :1] + mean) + epsilon)
         new[t] = rows[t] - summed * scale
-        out = pltpu.make_async_copy(new.at[t], new_ref.at[t], out_sem.at[n_chunk + t])
-        out.start()
-        ends.append(out)
-
+        pltpu.make_async_copy(new.at[t], new_ref.at[t], out_sem.at[n_chunk + t]).start()
+
+    take(0)
+    scatter(0)
+    far_home.wait()
+    spread(0)
+    take(1)
+    scatter(1)
+    swap_halves(0)
+    spread(1)
+    update(0)
+    swap_halves(1)
+    update(1)
+
+    lend_rows.wait_send()
+    pltpu.make_async_copy(lines, lines, s_send).wait()
+    pltpu.make_async_copy(shares, shares, w_send).wait()
+    lend_core.wait_send()
+    pltpu.make_async_copy(far_others, far_others, j_send).wait()
     for c in range(n_chunk):
-        all_of(pooled, 0, tabs, f_send.at[c]).wait()
+        bytes_of(n_shard - 2, 0, tabs, f_send.at[c]).wait()
+        bytes_of(near_both - 1, 0, tabs, e_send.at[c]).wait()
         part = pl.ds(c * SUB, SUB)
         pltpu.make_async_copy(inter.at[part], inter_ref.at[0, part], out_sem.at[c]).wait()
-    for c in range(n_chunk - 1):
-        all_of(pooled, 0, tabs, b_send.at[c]).wait()
+    for c in range(last):
+        bytes_of(direct - 1, 0, tabs, b_send.at[c]).wait()
     for t in range(tabs):
-        all_of(pooled, t, 1, b_send.at[last + t]).wait()
-        others = y_got.at[t, pl.ds(0, n_y - 1)]
-        pltpu.make_async_copy(others, others, y_send.at[t]).wait()
-        pltpu.make_async_copy(others, others, g_send.at[t]).wait()
-        ends[t].wait()
+        bytes_of(direct - 1, t, 1, b_send.at[last + t]).wait()
+        others(t, y_send.at[t]).wait()
+        others(t, g_send.at[t]).wait()
+        pltpu.make_async_copy(new.at[t], new_ref.at[t], out_sem.at[n_chunk + t]).wait()
 
 
 def local(n_shard, n_rep, emb_table, accumulated, touched, bag_slots, lengths, cotangent):
@@ -455,11 +659,26 @@
             pltpu.VMEM((tabs, n_y, half // n_y, dim), low),
             pltpu.VMEM((tabs, width, dim), low),
             pltpu.VMEM((tabs, width, dim), f32),
+            pltpu.VMEM((tabs * slots.shape[1], batch), jnp.int16),
+            pltpu.VMEM((tabs * slots.shape[1], batch), jnp.int16),
+            pltpu.VMEM((tabs, width, dim), low),
+            pltpu.VMEM((tabs, width, batch), low),
+            pltpu.VMEM((tabs, batch, dim), low),
+            pltpu.VMEM((tabs, batch, dim), low),
+            pltpu.VMEM((tabs, width, dim), low),
+            pltpu.VMEM((tabs, half, dim), low),
+            pltpu.VMEM((tabs, width, dim), f32),
+            pltpu.VMEM((tabs, half, dim), low),
+            pltpu.VMEM((n_y, tabs, half // n_y, dim), low),
+            pltpu.VMEM((tabs, half // n_y, dim), low),
+            pltpu.VMEM((tabs, half // n_y, dim), low),
             dma((3 + tabs,)),
             dma((n_chunk + tabs,)),
             *[dma((n_chunk,))] * 3,
             *[dma((n_chunk - 1 + tabs,))] * 3,
             *[dma((tabs,))] * 8,
+            *[dma((n_chunk,))] * 3,
+            *[dma] * 14,
         ],
         compiler_params=pltpu.CompilerParams(
             collective_id=0, has_side_effects=True, vmem_limit_bytes=56 << 20

time: 177 us -> 146 us (0.82)
  Pallas kernels: 171 us -> 141 us
    pallas_call x1, Pallas kernels: 171 us -> 141 us  [local(): pl.pallas_call(functools.partial(main_kernel, n_shard, n_rep, ring, n_chu...]
where the time goes in v3:
time: 146 us
  Pallas kernels  141 us (97%)
  local copies, waits for them, and re-layouts  4.57 us (3%)
    pallas_call x1, Pallas kernels, local(): pl.pallas_call(functools.partial(main_kernel, n_shard, n_rep, ring, n_chu...  141 us
    unnamed x2, local copies, waits for them, and re-layouts  4.57 us

profile of v3, /device:TPU:1, one launch (start us, length us, event | category | flops | bytes accessed | tf_op | source)
XLA Modules:
  0.0 146.2 jit_solution(2691443997143125306)
XLA Ops:
  0.6 141.0 %shard_map.77 = (bf16[1,32,128,128]{3,2,1,0:T(8,128)(2,1)}, f32[2,512,256]{2,1,0:T(8,128)}) custom-call(f32[2,2048,256]{2,1,0:T(8,128)} %table_ref.1, f32[2,2048]{1,0:T(2,128)} %acc_ref.1, s32[2,512]{1,0:T(2,128)} %touched_ref.1, s32[2,16,2048]{2,1,0:T(8,128)} %bitcast.3, s32[2,1,2048]{2,1,0:T(1,128)} %len_ref.1, bf16[1,32,128,128]{3,2,1,0:T(8,128)(2,1)} %cot_ref.1), custom_call_target="tpu_custom_call" | custom-call | tf_op jit(solution)/shard_map/pallas_call | solution.py:630
  141.6 2.3 %copy.10 = bf16[1,32,128,128]{3,2,1,0:T(8,128)(2,1)} copy(bf16[1,32,128,128]{3,2,1,0:T(8,128)(2,1)} %get-tuple-element.4) | data formatting | bytes 2097152
  143.9 2.3 %copy.11 = f32[2,512,256]{2,1,0:T(8,128)} copy(f32[2,512,256]{2,1,0:T(8,128)} %get-tuple-element.5) | data formatting | bytes 2097152

commit v4 on v3

--- a/solution.py
+++ b/solution.py
@@ -50,7 +50,6 @@
     near_x = (0, 1, -1, 2)
     far_x = (4, 5, 3, 6)
     dgot[...] = jnp.zeros_like(dgot)
-    dfar[...] = jnp.zeros_like(dfar)
 
     loads = [
         pltpu.make_async_copy(touched_ref, touched, in_sem.at[0]),
@@ -104,9 +103,6 @@
             for c in range(n_chunk):
                 lanes = pl.ds(pl.multiple_of(c * span + r * line, line), line)
                 slots[t, :, lanes] = ids[:, c * line : (c + 1) * line]
-                slots_out[pl.ds(t * deep, deep), lanes] = ids[:, c * line : (c + 1) * line].astype(
-                    jnp.int16
-                )
         return carry
 
     lax.fori_loop(0, n_z, sort_slots, 0)
@@ -180,21 +176,33 @@
     )
     lend_rows.start()
 
-    def lend_slots(i, carry):
-        far = z_pair(i, turn)[1]
+    pairs = n_z // 4
+    far_span = pairs * line
+    column = lax.broadcasted_iota(jnp.int32, (deep, line), 1) // SUB
+    far_lane = lax.rem(turn * (column - x) + 2 * ring + 5, ring) < ring // 2
+
+    def lend_slots(p, carry):
         for c in range(n_chunk):
-            lanes = pl.ds(pl.multiple_of(c * span + far * line, line), line)
-            pltpu.make_async_remote_copy(
-                src_ref=slots_out.at[:, lanes],
-                dst_ref=slots_far.at[:, lanes],
-                send_sem=s_send,
-                recv_sem=s_recv,
-                device_id={"shard": opposite},
-                device_id_type=MESH,
-            ).start()
-        return carry
-
-    lax.fori_loop(0, n_z // 2, lend_slots, 0)
+            lanes = pl.ds(pl.multiple_of(c * far_span + p * line, line), line)
+            for t in range(tabs):
+                first, second = (
+                    slots[t, :, pl.ds(pl.multiple_of(c * span + r * line, line), line)]
+                    for r in (z_pair(2 * p, turn)[1], z_pair(2 * p + 1, turn)[1])
+                )
+                packed = jnp.where(far_lane, first, pltpu.roll(second, line // 2, 1))
+                slots_out[pl.ds(t * deep, deep), lanes] = packed.astype(jnp.int16)
+        return carry
+
+    lax.fori_loop(0, pairs, lend_slots, 0)
+    lent_slots = pltpu.make_async_remote_copy(
+        src_ref=slots_out,
+        dst_ref=slots_far,
+        send_sem=s_send,
+        recv_sem=s_recv,
+        device_id={"shard": opposite},
+        device_id_type=MESH,
+    )
+    lent_slots.start()
 
     def send(src, dst, dest, sent, landed, kept):
         @pl.when(dest == me)
@@ -235,24 +243,24 @@
             out(pair[0], x_at(far_x[j], turn))
         return carry
 
-    def forward_far(i, carry, c):
-        near, far = z_pair(i, turn)
-        first = pl.multiple_of(c * span + far * line, line)
+    def forward_far(p, carry, c):
+        first = pl.multiple_of(c * far_span + p * line, line)
         for t in range(tabs):
-            ids = slots_far[pl.ds(t * deep, deep), pl.ds(c * span + near * line, line)]
-            ids = pltpu.roll(ids.astype(jnp.int32), line // 2, 1)
+            ids = slots_far[pl.ds(t * deep, deep), pl.ds(first, line)].astype(jnp.int32)
             count(ids, t, counts_far, first)
             pool(t, first, counts_far, low_far, pooled_far)
         for j in range(ring // 2):
-            column = x_at(far_x[j], turn)
-            send(
-                pooled_far.at[:, pl.ds(c * span + (far * ring + column) * SUB, SUB), :],
-                got.at[pl.ds(opposite * tabs, tabs), pl.ds(c * SUB, SUB), :],
-                near * ring + lax.rem(column + ring // 2, ring),
-                f_send.at[c],
-                f_recv.at[c],
-                f_own.at[c],
-            )
+            dest_x = x_at(near_x[j], turn)
+            for odd in range(2):
+                place = lax.rem(dest_x + odd * (ring // 2), ring)
+                send(
+                    pooled_far.at[:, pl.ds(first + place * SUB, SUB), :],
+                    got.at[pl.ds(opposite * tabs, tabs), pl.ds(c * SUB, SUB), :],
+                    z_pair(2 * p + odd, turn)[0] * ring + dest_x,
+                    f_send.at[c],
+                    f_recv.at[c],
+                    f_own.at[c],
+                )
         return carry
 
     def count_later(r, carry, c):
@@ -289,12 +297,12 @@
         device_id_type=MESH,
     )
     lend_core.start()
-    lines = slots_out.at[:, pl.ds(0, n_chunk * line * (n_z // 2))]
-    pltpu.make_async_copy(lines, lines, s_recv).wait()
+    lax.fori_loop(0, n_z // 4, functools.partial(forward, c=1), 0)
+    lent_slots.wait_recv()
     lend_core.wait_recv()
-    lax.fori_loop(0, n_z // 2, functools.partial(forward_far, c=0), 0)
-    lax.fori_loop(0, n_z // 2, functools.partial(forward, c=1), 0)
-    lax.fori_loop(0, n_z // 2, functools.partial(forward_far, c=1), 0)
+    lax.fori_loop(0, pairs, functools.partial(forward_far, c=0), 0)
+    lax.fori_loop(n_z // 4, n_z // 2, functools.partial(forward, c=1), 0)
+    lax.fori_loop(0, pairs, functools.partial(forward_far, c=1), 0)
 
     loads[1].wait()
 
@@ -329,6 +337,28 @@
 
     near_both = (n_z // 2) * (ring // 2)
     direct = n_shard - near_both
+
+    def backward(i, carry, c, t):
+        pair = z_pair(i, -turn)
+        k = t * n_chunk + c
+
+        def out(r, column):
+            dest = r * ring + column
+            send(
+                dsend.at[pl.ds(dest * tabs + t, 1), pl.ds(c * SUB, SUB), :],
+                dgot.at[pl.ds(t, 1), pl.ds(c * span + me * SUB, SUB), :],
+                dest,
+                b_send.at[k],
+                b_recv.at[k],
+                b_own.at[k],
+            )
+
+        for u in range(ring // 2):
+            out(pair[0], x_at(near_x[u], -turn))
+            out(pair[1], x_at(-near_x[u], turn))
+            out(pair[0], x_at(far_x[u], -turn))
+        return carry
+
     for c in range(n_chunk):
         bytes_of(n_shard - 2, 0, tabs, f_recv.at[c]).wait()
         bytes_of(2, 0, tabs, f_own.at[c]).wait()
@@ -359,8 +389,6 @@
         lax.fori_loop(0, SUB // 4, sample, 0)
         pltpu.make_async_copy(inter.at[part], inter_ref.at[0, part], out_sem.at[c]).start()
 
-        split = [(0, tabs)] if c < n_chunk - 1 else [(t, 1) for t in range(tabs)]
-
         def to_tables(g, carry, part=part):
             first = pl.multiple_of(g * SUB, SUB)
             dsend[pl.ds(first, SUB), part, :] = swap_tile(dmine[part, pl.ds(first, SUB), :])
@@ -370,12 +398,13 @@
 
         def backward_far(i, carry, c=c):
             near, far = z_pair(i, -turn)
+            place = lax.rem(x + lax.rem(i, 2) * (ring // 2), ring)
             for j in range(ring // 2):
-                column = x_at(far_x[j], -turn)
+                home_x = x_at(far_x[j], -turn)
                 send(
-                    dsend.at[pl.ds((far * ring + column) * tabs, tabs), pl.ds(c * SUB, SUB), :],
-                    dfar.at[:, pl.ds(c * span + opposite * SUB, SUB), :],
-                    near * ring + lax.rem(column + ring // 2, ring),
+                    dsend.at[pl.ds((far * ring + home_x) * tabs, tabs), pl.ds(c * SUB, SUB), :],
+                    dfar.at[:, pl.ds(c * far_span + i // 2 * line + place * SUB, SUB), :],
+                    near * ring + lax.rem(home_x + ring // 2, ring),
                     e_send.at[c],
                     e_recv.at[c],
                     e_own.at[c],
@@ -384,29 +413,9 @@
 
         lax.fori_loop(0, n_z // 2, backward_far, 0)
 
-        for j, (t0, count_t) in enumerate(split):
-
-            def backward(i, carry, c=c, k=c + j, t0=t0, count_t=count_t):
-                pair = z_pair(i, -turn)
-
-                def out(r, column):
-                    dest = r * ring + column
-                    send(
-                        dsend.at[pl.ds(dest * tabs + t0, count_t), pl.ds(c * SUB, SUB), :],
-                        dgot.at[pl.ds(t0, count_t), pl.ds(c * span + me * SUB, SUB), :],
-                        dest,
-                        b_send.at[k],
-                        b_recv.at[k],
-                        b_own.at[k],
-                    )
-
-                for u in range(ring // 2):
-                    out(pair[0], x_at(near_x[u], -turn))
-                    out(pair[1], x_at(-near_x[u], turn))
-                    out(pair[0], x_at(far_x[u], -turn))
-                return carry
-
-            lax.fori_loop(0, n_z // 2, backward, 0)
+        for t in range(tabs):
+            for sent in [c] if t == 0 else range(n_chunk) if c == n_chunk - 1 else []:
+                lax.fori_loop(0, n_z // 2, functools.partial(backward, c=sent, t=t), 0)
 
     def gradient(t, c):
         def rows_of(i, carry):
@@ -432,27 +441,22 @@
     here = pl.ds(pl.multiple_of(core * half + y * piece, piece), piece)
     last = n_chunk - 1
 
+    def take(t, c):
+        bytes_of(direct - 1, t, 1, b_recv.at[t * n_chunk + c]).wait()
+        bytes_of(1, t, 1, b_own.at[t * n_chunk + c]).wait()
+        gradient(t, c)
+
     for c in range(last):
-        bytes_of(direct - 1, 0, tabs, b_recv.at[c]).wait()
-        bytes_of(1, 0, tabs, b_own.at[c]).wait()
-        for t in range(tabs):
-            gradient(t, c)
+        take(0, c)
 
     for c in range(n_chunk):
         bytes_of(near_both - 1, 0, tabs, e_recv.at[c]).wait()
         bytes_of(1, 0, tabs, e_own.at[c]).wait()
     for t in range(tabs):
         for rows_at in range(0, width, 256):
-            total = jnp.zeros((256, dim), jnp.float32)
-            for i in range(n_z // 2):
-                far = z_pair(i, turn)[1]
-                for c in range(n_chunk):
-                    block = pl.ds(pl.multiple_of(c * span + far * line, line), line)
-                    total = total + jnp.dot(
-                        counts_far[t, rows_at : rows_at + 256, block],
-                        dfar[t, block, :],
-                        preferred_element_type=jnp.float32,
-                    )
+            total = jnp.dot(
+                counts_far[t, rows_at : rows_at + 256, :], dfar[t], preferred_element_type=jnp.float32
+            )
             far_kept[t, rows_at : rows_at + 256, :] = total
             far_low[t, rows_at : rows_at + 256, :] = total.astype(jnp.bfloat16)
     far_trade = pltpu.make_async_remote_copy(
@@ -483,11 +487,6 @@
     lax.fori_loop(1, n_y, far_scatter, 0)
     far_y[y] = far_half_low[:, pl.ds(pl.multiple_of(y * piece, piece), piece), :]
     far_others = far_y.at[pl.ds(0, n_y - 1)]
-    pltpu.make_async_copy(far_others, far_others, j_recv).wait()
-    total = far_y[0].astype(jnp.float32)
-    for i in range(1, n_y):
-        total = total + far_y[i].astype(jnp.float32)
-    far_out[...] = total.astype(jnp.bfloat16)
     far_home = pltpu.make_async_remote_copy(
         src_ref=far_out,
         dst_ref=far_in,
@@ -496,7 +495,14 @@
         device_id={"shard": opposite},
         device_id_type=MESH,
     )
-    far_home.start()
+
+    def send_home():
+        pltpu.make_async_copy(far_others, far_others, j_recv).wait()
+        total = far_y[0].astype(jnp.float32)
+        for i in range(1, n_y):
+            total = total + far_y[i].astype(jnp.float32)
+        far_out[...] = total.astype(jnp.bfloat16)
+        far_home.start()
 
     def trade(t):
         return pltpu.make_async_remote_copy(
@@ -521,12 +527,6 @@
     def others(t, sem):
         view = y_got.at[t, pl.ds(0, n_y - 1)]
         return pltpu.make_async_copy(view, view, sem)
-
-    def take(t):
-        bytes_of(direct - 1, t, 1, b_recv.at[last + t]).wait()
-        bytes_of(1, t, 1, b_own.at[last + t]).wait()
-        gradient(t, last)
-        trade(t).start()
 
     def scatter(t):
         trade(t).wait()
@@ -582,11 +582,16 @@
         new[t] = rows[t] - summed * scale
         pltpu.make_async_copy(new.at[t], new_ref.at[t], out_sem.at[n_chunk + t]).start()
 
-    take(0)
+    take(0, last)
+    trade(0).start()
+    send_home()
     scatter(0)
+    for c in range(last):
+        take(1, c)
     far_home.wait()
     spread(0)
-    take(1)
+    take(1, last)
+    trade(1).start()
     scatter(1)
     swap_halves(0)
     spread(1)
@@ -595,7 +600,7 @@
     update(1)
 
     lend_rows.wait_send()
-    pltpu.make_async_copy(lines, lines, s_send).wait()
+    lent_slots.wait_send()
     pltpu.make_async_copy(shares, shares, w_send).wait()
     lend_core.wait_send()
     pltpu.make_async_copy(far_others, far_others, j_send).wait()
@@ -604,13 +609,34 @@
         bytes_of(near_both - 1, 0, tabs, e_send.at[c]).wait()
         part = pl.ds(c * SUB, SUB)
         pltpu.make_async_copy(inter.at[part], inter_ref.at[0, part], out_sem.at[c]).wait()
-    for c in range(last):
-        bytes_of(direct - 1, 0, tabs, b_send.at[c]).wait()
     for t in range(tabs):
-        bytes_of(direct - 1, t, 1, b_send.at[last + t]).wait()
+        for c in range(n_chunk):
+            bytes_of(direct - 1, t, 1, b_send.at[t * n_chunk + c]).wait()
         others(t, y_send.at[t]).wait()
         others(t, g_send.at[t]).wait()
         pltpu.make_async_copy(new.at[t], new_ref.at[t], out_sem.at[n_chunk + t]).wait()
+
+
+def hand_over(interaction, new_rows):
+    def kernel(inter, new, inter_out, new_out):
+        inter_out[...] = inter[...]
+        new_out[...] = new[...]
+
+    _, own, n_tab, _ = interaction.shape
+    tabs, width, dim = new_rows.shape
+    steps = 4
+    specs = (
+        pl.BlockSpec((1, own // steps, n_tab, n_tab), lambda i: (0, i, 0, 0)),
+        pl.BlockSpec((tabs, width // steps, dim), lambda i: (0, i, 0)),
+    )
+    return pl.pallas_call(
+        kernel,
+        grid=(steps,),
+        out_shape=tuple(jax.ShapeDtypeStruct(a.shape, a.dtype) for a in (interaction, new_rows)),
+        in_specs=specs,
+        out_specs=specs,
+        compiler_params=pltpu.CompilerParams(vmem_limit_bytes=60 << 20),
+    )(interaction, new_rows)
 
 
 def local(n_shard, n_rep, emb_table, accumulated, touched, bag_slots, lengths, cotangent):
@@ -627,7 +653,7 @@
     dma = pltpu.SemaphoreType.DMA
     low = jnp.bfloat16
     f32 = jnp.float32
-    return pl.pallas_call(
+    results = pl.pallas_call(
         functools.partial(main_kernel, n_shard, n_rep, ring, n_chunk),
         out_shape=(
             jax.ShapeDtypeStruct((1, own, n_tab, n_tab), low),
@@ -659,12 +685,12 @@
             pltpu.VMEM((tabs, n_y, half // n_y, dim), low),
             pltpu.VMEM((tabs, width, dim), low),
             pltpu.VMEM((tabs, width, dim), f32),
-            pltpu.VMEM((tabs * slots.shape[1], batch), jnp.int16),
-            pltpu.VMEM((tabs * slots.shape[1], batch), jnp.int16),
+            pltpu.VMEM((tabs * slots.shape[1], batch // 4), jnp.int16),
+            pltpu.VMEM((tabs * slots.shape[1], batch // 4), jnp.int16),
             pltpu.VMEM((tabs, width, dim), low),
-            pltpu.VMEM((tabs, width, batch), low),
-            pltpu.VMEM((tabs, batch, dim), low),
-            pltpu.VMEM((tabs, batch, dim), low),
+            pltpu.VMEM((tabs, width, batch // 4), low),
+            pltpu.VMEM((tabs, batch // 4, dim), low),
+            pltpu.VMEM((tabs, batch // 4, dim), low),
             pltpu.VMEM((tabs, width, dim), low),
             pltpu.VMEM((tabs, half, dim), low),
             pltpu.VMEM((tabs, width, dim), f32),
@@ -675,7 +701,7 @@
             dma((3 + tabs,)),
             dma((n_chunk + tabs,)),
             *[dma((n_chunk,))] * 3,
-            *[dma((n_chunk - 1 + tabs,))] * 3,
+            *[dma((n_chunk * tabs,))] * 3,
             *[dma((tabs,))] * 8,
             *[dma((n_chunk,))] * 3,
             *[dma] * 14,
@@ -684,6 +710,7 @@
             collective_id=0, has_side_effects=True, vmem_limit_bytes=56 << 20
         ),
     )(emb_table, accumulated, touched, slots, lengths, cotangent)
+    return hand_over(*results)
 
 
 def solution(mesh):

time: 146 us -> 129 us (0.88); the launches traced: 146 us -> 127 us
  Pallas kernels: 141 us -> 127 us
  local copies, waits for them, and re-layouts: 4.57 us -> 0 us
    pallas_call x1, Pallas kernels: 141 us -> 123 us  [local(): pl.pallas_call(functools.partial(main_kernel, n_shard, n_rep, ring, n_chu...]
    unnamed x2 -> x0, local copies, waits for them, and re-layouts: 4.57 us -> none
    pallas_call x0 -> x1, Pallas kernels: none -> 3.75 us  [hand_over(): pl.pallas_call(kernel, grid=(steps,), out_shape=tuple((jax.ShapeDtypeStru...]
where the time goes in v4:
time: 129 us; the launch traced here: 127 us
  Pallas kernels  127 us (98%)
    pallas_call x1, Pallas kernels, local(): pl.pallas_call(functools.partial(main_kernel, n_shard, n_rep, ring, n_chu...  123 us
    pallas_call x1, Pallas kernels, hand_over(): pl.pallas_call(kernel, grid=(steps,), out_shape=tuple((jax.ShapeDtypeStru...  3.75 us

profile of v4, /device:TPU:1, one launch (start us, length us, event | category | flops | bytes accessed | tf_op | source)
XLA Modules:
  0.0 127.2 jit_solution(9828085425748146482)
XLA Ops:
  0.6 122.8 %shard_map.77 = (bf16[1,32,128,128]{3,2,1,0:T(8,128)(2,1)}, f32[2,512,256]{2,1,0:T(8,128)}) custom-call(f32[2,2048,256]{2,1,0:T(8,128)} %table_ref.1, f32[2,2048]{1,0:T(2,128)} %acc_ref.1, s32[2,512]{1,0:T(2,128)} %touched_ref.1, s32[2,16,2048]{2,1,0:T(8,128)} %bitcast.3, s32[2,1,2048]{2,1,0:T(1,128)} %len_ref.1, bf16[1,32,128,128]{3,2,1,0:T(8,128)(2,1)} %cot_ref.1), custom_call_target="tpu_custom_call" | custom-call | tf_op jit(solution)/shard_map/pallas_call | solution.py:656
  123.4 3.8 %shard_map.78 = (bf16[1,32,128,128]{3,2,1,0:T(8,128)(2,1)}, f32[2,512,256]{2,1,0:T(8,128)}) custom-call(bf16[1,32,128,128]{3,2,1,0:T(8,128)(2,1)} %get-tuple-element.4.inter, f32[2,512,256]{2,1,0:T(8,128)} %get-tuple-element.5.new), custom_call_target="tpu_custom_call" | custom-call | tf_op jit(solution)/shard_map/pallas_call | solution.py:632
